TPU v7x, 128 devices: a whole 4x4x4 slice. The times are simulated.
128 devices in a mesh: gx: 16 (over z, x), gy: 8 (over y, core).
Axes of the slice: x: 4, y: 4, z: 4, core: 2. Of those that a mesh axis runs over, the one named last changes fastest.
Arguments:
- atm_fields: float32 [8, 262144], P(None, ('gx', 'gy')), may hold values from -6 to 6
- send_cols: int32 [128, 9, 512], P(('gx', 'gy')), may hold values from 0 to 2047
- pair_count: int32 [128, 9], P(('gx', 'gy')), may hold values from 0 to 512, as said below
- remap_slot: int32 [4, 1024, 1024], P(None, 'gx', 'gy'), may hold values from 0 to 4607, as said below
- remap_weight: float32 [4, 1024, 1024], P(None, 'gx', 'gy'), may hold values from 0.05 to 0.5
- land_mask: int32 [1024, 1024], P('gx', 'gy'), may hold values 0 or 1
- tracers: float32 [2, 32, 1024, 1024], P(None, None, 'gx', 'gy'), may hold values from -6 to 6
- kappa: float32 [32, 1024, 1024], P(None, 'gx', 'gy'), may hold values from 0.02 to 0.2
Outputs:
- atm_flux: float32 [4, 262144], P(None, ('gx', 'gy'))
- tracers_out: float32 [2, 32, 1024, 1024], P(None, None, 'gx', 'gy')
Inputs may be any that keep to these rules, and one draw needn't show every extreme that they name: pair_count[s, o] is 0 exactly where offset o leads from device s out of the device grid; inside it, it is 512 for offsets 4 and 8 and between 128 and 512 for the others. So a device sends to and receives from its own position and its eight neighbours in the device grid only. `remap_slot`: every intersection names an offset o whose source device lies inside the device grid and a slot j below pair_count of that source and offset.
All inputs are finite; a program needn't handle non-finite values. No bound on the sum of `land_mask` on one device may be relied on, other than what follows from the above.
Results may differ from a plain program's by a relative error of at most 0.00002.
Values sent between devices are 32-bit elements; how exact they have to be, the bound alone decides.
A program may use at most 128 MiB of HBM per device.

v0:
```python
import jax
import jax.numpy as jnp
from jax import lax
from jax.sharding import PartitionSpec as P

STEPS = 4


vertical_mix = 0.05
force_rate = 0.05


def padded_2(shard, sides, width):
    for axis, dim in sides:
        size, length = (lax.axis_size(axis), shard.shape[dim])
        up = [(i, (i + 1) % size) for i in range(size - 1)]
        down = [(j, i) for i, j in up]
        last = lax.slice_in_dim(shard, length - width, length, axis=dim)
        first = lax.slice_in_dim(shard, 0, width, axis=dim)
        before = lax.ppermute(last, axis, up)
        after = lax.ppermute(first, axis, down)
        shard = jnp.concatenate([before, shard, after], axis=dim)
    return shard


def interface_transfer_rate(
    quantity_grids, topmost_warmth, topmost_saltiness, ocean_cell_indicator
):
    breeze_speed = jnp.sqrt(
        quantity_grids[0] * quantity_grids[0] + quantity_grids[1] * quantity_grids[1] + 1.0
    )
    thermal_energy_gain = (
        breeze_speed * (quantity_grids[2] - topmost_warmth) + quantity_grids[4] + quantity_grids[5]
    )
    water = breeze_speed * (quantity_grids[3] - 0.2 * topmost_saltiness) - quantity_grids[6]
    stress_x = breeze_speed * quantity_grids[0] + 0.5 * quantity_grids[7]
    stress_y = breeze_speed * quantity_grids[1] - 0.5 * quantity_grids[7]
    return jnp.stack([thermal_energy_gain, water, stress_x, stress_y]) * ocean_cell_indicator


def update(cpad, kpad, ocean_cell_indicator, forcing):
    center = cpad[:, :, 1:-1, 1:-1]
    kc = kpad[:, 1:-1, 1:-1]
    lap = jnp.sqrt(kc * kpad[:, 2:, 1:-1]) * (cpad[:, :, 2:, 1:-1] - center)
    lap = lap + jnp.sqrt(kc * kpad[:, :-2, 1:-1]) * (cpad[:, :, :-2, 1:-1] - center)
    lap = lap + jnp.sqrt(kc * kpad[:, 1:-1, 2:]) * (cpad[:, :, 1:-1, 2:] - center)
    lap = lap + jnp.sqrt(kc * kpad[:, 1:-1, :-2]) * (cpad[:, :, 1:-1, :-2] - center)
    above = jnp.concatenate([center[:, :1], center[:, :-1]], 1)
    below = jnp.concatenate([center[:, 1:], center[:, -1:]], 1)
    fresh = center + lap + vertical_mix * (above + below - 2.0 * center) * ocean_cell_indicator
    return jnp.concatenate([fresh[:, :1] + forcing[:, None], fresh[:, 1:]], 1)


def per_device(
    atm_fields, send_cols, pair_count, remap_slot, remap_weight, land_mask, tracers, kappa
):
    nfield = atm_fields.shape[0]
    ncols = atm_fields.shape[1]
    slots = send_cols.shape[2]
    nflux = 4
    slot_iota = lax.broadcasted_iota(jnp.int32, (9, slots), 1)
    live = (slot_iota < pair_count[0][:, None]).astype(jnp.float32)
    columns = send_cols[0]
    outgoing = atm_fields[:, columns] * live
    grid_out = jnp.moveaxis(outgoing, 1, 0).reshape(3, 3, nfield, slots)
    padded = padded_2(grid_out, (("gx", 0), ("gy", 1)), 1)
    arrived = padded[::-2, ::-2]
    received = jnp.moveaxis(arrived.reshape(9, nfield, slots), 1, 0).reshape(nfield, 9 * slots)
    ocean_cell_indicator = land_mask.astype(jnp.float32)
    remapped = jnp.zeros((nfield,) + land_mask.shape, jnp.float32)
    for k in range(remap_slot.shape[0]):
        remapped = remapped + remap_weight[k] * received[:, remap_slot[k]]
    flux = interface_transfer_rate(remapped, tracers[0, 0], tracers[1, 0], ocean_cell_indicator)
    contrib = jnp.zeros((nflux, 9 * slots), jnp.float32)
    for k in range(remap_slot.shape[0]):
        contrib = contrib.at[:, remap_slot[k]].add(remap_weight[k] * flux)
    grid_back = jnp.moveaxis(contrib.reshape(nflux, 9, slots), 1, 0).reshape(3, 3, nflux, slots)
    padded_back = padded_2(grid_back[::-1, ::-1], (("gx", 0), ("gy", 1)), 1)
    returned = padded_back[::2, ::2]
    returned = jnp.moveaxis(returned.reshape(9, nflux, slots), 1, 0) * live
    atm_flux = jnp.zeros((nflux, ncols), jnp.float32).at[:, columns].add(returned)
    forcing = force_rate * jnp.stack([flux[0], -flux[1]])
    kmask = kappa * ocean_cell_indicator[None]
    state = tracers
    rim_width = 1
    kpad = padded_2(kmask, (("gx", 1), ("gy", 2)), rim_width)
    for step in range(STEPS):
        cpad = padded_2(state, (("gx", 2), ("gy", 3)), 1)
        state = update(cpad, kpad, ocean_cell_indicator, forcing)
    return (atm_flux, state)


def solution(mesh):
    return jax.shard_map(
        per_device,
        mesh=mesh,
        in_specs=(
            P(None, ("gx", "gy")),
            P(("gx", "gy"), None, None),
            P(("gx", "gy"), None),
            P(None, "gx", "gy"),
            P(None, "gx", "gy"),
            P("gx", "gy"),
            P(None, None, "gx", "gy"),
            P(None, "gx", "gy"),
        ),
        out_specs=(P(None, ("gx", "gy")), P(None, None, "gx", "gy")),
        check_vma=False,
    )
```

profile of v0, /device:TPU:105, one launch (start us, length us, event | category | flops | bytes accessed | tf_op | source)
XLA Modules:
  0.0 700.7 jit_solution(3536764725923189226)
XLA Ops:
  2.6 7.3 %gather_fusion = f32[4608,8]{1,0:T(8,128)S(1)} fusion(f32[8,2048]{0,1:T(8,128)S(1)} %copy.110, s32[5120]{0:T(1024)S(1)} %pad_clamp_fusion), kind=kCustom, calls=%fused_computation | custom fusion | bytes 313344 | tf_op jit(solution)/shard_map/gather | solution.py:64
  20.0 5.5 collective-permute-start.9
  42.2 8.4 %fusion.96 = (f32[2,31,64,128]{2,1,3,0:T(8,128)}, f32[2,31,64,128]{2,1,3,0:T(8,128)}) fusion(f32[2,32,64,128]{2,1,3,0:T(8,128)} %copy.145), kind=kLoop, calls=%fused_computation.245 | loop fusion | bytes 8126464 | tf_op jit(solution)/shard_map/slice | solution.py:49
  88.6 5.1 copy.127
  110.2 18.5 %fusion.61 = f32[2,32,64,128]{2,1,3,0:T(8,128)} fusion(f32[2,32,64,128]{2,1,3,0:T(8,128)S(1)} %copy-done.6, f32[2,32,66,1]{2,1,3,0:T(8,128)S(1)} %collective-permute-done.15, f32[2,32,1,128]{2,1,3,0:T(8,128)} %copy.127, f32[2,32,1,128]{2,1,3,0:T(8,128)} %copy.131, f32[2,32,66,1]{2,1,3,0:T(8,128)S(1)} %collective-permute-done.13, ...), kind=kLoop, calls=%fused_computation.123 | loop fusion | flops 14155776 | bytes 12715008 | tf_op jit(solution)/shard_map/add | solution.py:50
  136.5 29.6 %gather_fusion.4 = f32[8192,8]{1,0:T(8,128)} fusion(f32[8,4608]{0,1:T(8,128)} %bitcast.96, s32[8192]{0:T(1024)S(1)} %copy-done.30), kind=kCustom, calls=%fused_computation.4 | custom fusion | bytes 557056 | tf_op jit(solution)/shard_map/gather | solution.py:72
  168.9 29.6 %gather_fusion.3 = f32[8192,8]{1,0:T(8,128)} fusion(f32[8,4608]{0,1:T(8,128)} %bitcast.97, s32[8192]{0:T(1024)S(1)} %copy-done.29), kind=kCustom, calls=%fused_computation.3 | custom fusion | bytes 557056 | tf_op jit(solution)/shard_map/gather | solution.py:72
  201.3 29.6 %gather_fusion.2 = f32[8192,8]{1,0:T(8,128)} fusion(f32[8,4608]{0,1:T(8,128)} %bitcast.98, s32[8192]{0:T(1024)S(1)} %get-tuple-element.69), kind=kCustom, calls=%fused_computation.2 | custom fusion | bytes 557056 | tf_op jit(solution)/shard_map/gather | solution.py:72
  233.7 29.6 %gather_fusion.1 = f32[8192,8]{1,0:T(8,128)} fusion(f32[8,4608]{0,1:T(8,128)} %bitcast.99, s32[8192]{0:T(1024)S(1)} %copy-done.28), kind=kCustom, calls=%fused_computation.1 | custom fusion | bytes 557056 | tf_op jit(solution)/shard_map/gather | solution.py:72
  271.4 7.4 %fusion.19 = (f32[2,32,1,128]{2,1,3,0:T(8,128)}, f32[2,32,1,128]{2,1,3,0:T(8,128)}) fusion(f32[2,1,64,128]{2,1,3,0:T(1,128)S(1)} %get-tuple-element.33, f32[2,31,64,128]{2,1,3,0:T(8,128)} %slice.449), kind=kLoop, calls=%fused_computation.44 | loop fusion | flops 16384 | bytes 2162688 | tf_op jit(solution)/shard_map/concatenate | solution.py:51
  292.3 46.0 %scatter_custom_fusion = f32[4,4608]{0,1:T(8,128)} fusion(s32[8192]{0:T(1024)} %get-tuple-element.59, f32[8192,4]{1,0:T(8,128)} %bitcast.108, f32[]{:T(128)} %constant.9.clone.1), kind=kCustom, calls=%fused_computation.143 | custom fusion | flops 32768 | bytes 74240 | tf_op jit(solution)/shard_map/scatter-add | solution.py:76
  338.3 42.9 %scatter_fusion = f32[4,4608]{0,1:T(8,128)} fusion(f32[4,4608]{0,1:T(8,128)} %scatter_custom_fusion, s32[8192]{0:T(1024)S(1)} %copy-done.27, f32[8192,4]{1,0:T(8,128)} %bitcast.107), kind=kCustom, calls=%fused_computation.6 | custom fusion | flops 32768 | bytes 425984 | tf_op jit(solution)/shard_map/scatter-add | solution.py:76
  381.3 42.9 %scatter_fusion.1 = f32[4,4608]{0,1:T(8,128)} fusion(f32[4,4608]{0,1:T(8,128)} %scatter_fusion, s32[8192]{0:T(1024)S(1)} %copy-done.26, f32[8192,4]{1,0:T(8,128)} %bitcast.106), kind=kCustom, calls=%fused_computation.7 | custom fusion | flops 32768 | bytes 425984 | tf_op jit(solution)/shard_map/scatter-add | solution.py:76
  424.2 42.9 %scatter_fusion.2 = f32[4,4608]{0,1:T(8,128)} fusion(f32[4,4608]{0,1:T(8,128)} %scatter_fusion.1, s32[8192]{0:T(1024)S(1)} %copy-done.25, f32[8192,4]{1,0:T(8,128)} %bitcast.105), kind=kCustom, calls=%fused_computation.8 | custom fusion | flops 32768 | bytes 425984 | tf_op jit(solution)/shard_map/scatter-add | solution.py:76
  469.5 5.8 collective-permute-start.5
  489.9 4.9 copy.154
  511.5 18.6 %fusion.17 = f32[2,32,64,128]{2,1,3,0:T(8,128)} fusion(f32[2,1,64,128]{2,1,3,0:T(1,128)S(1)} %get-tuple-element.33, f32[2,32,66,1]{2,1,3,0:T(8,128)S(1)} %collective-permute-done.19, f32[2,32,1,128]{2,1,3,0:T(8,128)} %copy.154, f32[2,32,1,128]{2,1,3,0:T(8,128)} %copy.156, f32[2,31,64,128]{2,1,3,0:T(8,128)S(1)} %copy-done.1, ...), kind=kLoop, calls=%fused_computation.42 | loop fusion | flops 16777216 | bytes 10617856 | tf_op jit(solution)/shard_map/add | solution.py:50
  543.0 5.7 collective-permute-start.20
  554.4 4.9 fusion.13
  577.8 18.9 %fusion.10 = f32[2,32,64,128]{2,1,3,0:T(8,128)} fusion(f32[2,1,64,128]{2,1,3,0:T(1,128)S(1)} %get-tuple-element.31, f32[2,32,66,1]{2,1,3,0:T(8,128)S(1)} %collective-permute-done.23, f32[2,32,1,128]{2,1,3,0:T(8,128)} %copy.160, f32[2,32,1,128]{2,1,3,0:T(8,128)} %copy.162, f32[2,31,64,128]{2,1,3,0:T(8,128)S(1)} %copy-done.3, ...), kind=kLoop, calls=%fused_computation.35 | loop fusion | flops 16777216 | bytes 10617856 | tf_op jit(solution)/shard_map/add | solution.py:50
  610.3 5.7 collective-permute-start.24
  624.4 25.8 %scatter_custom_fusion.4 = f32[4,2048]{0,1:T(8,128)S(1)} fusion(s32[4608]{0:T(1024)} %copy-done.32, f32[4608,4]{1,0:T(8,128)} %bitcast.110, f32[]{:T(128)} %constant.9.clone.1), kind=kCustom, calls=%fused_computation.163 | custom fusion | flops 18432 | bytes 33280 | tf_op jit(solution)/shard_map/scatter-add | solution.py:81
  655.7 5.2 copy.168
  669.9 18.9 %fusion.3 = f32[2,32,64,128]{2,1,3,0:T(8,128)} fusion(f32[2,1,64,128]{2,1,3,0:T(1,128)S(1)} %get-tuple-element.29, f32[2,32,66,1]{2,1,3,0:T(8,128)S(1)} %collective-permute-done.27, f32[2,32,1,128]{2,1,3,0:T(8,128)} %copy.166, f32[2,32,1,128]{2,1,3,0:T(8,128)} %copy.168, f32[2,31,64,128]{2,1,3,0:T(8,128)S(1)} %copy-done.5, ...), kind=kLoop, calls=%fused_computation.28 | loop fusion | flops 16777216 | bytes 10617856 | tf_op jit(solution)/shard_map/add | solution.py:50
  (218 shorter events, 239.2 us)
Async XLA Ops:
  12.1 91.5 %collective-permute-start.1 = (f32[1,3,8,512]{3,2,1,0:T(8,128)}, f32[1,3,8,512]{3,2,1,0:T(8,128)}, u32[]{:S(2)}, u32[]{:S(2)}) collective-permute-start(f32[1,3,8,512]{3,2,1,0:T(8,128)} %get-tuple-element.54), channel_id=1, source_target_pairs={{8,0},{16,8},{24,16},{32,24},{40,32},{48,40},{56,48},{64,56},{72,6... | collective-permute-start | bytes 147464 | tf_op jit(solution)/shard_map/ppermute | solution.py:21
  16.3 87.3 %collective-permute-start = (f32[1,3,8,512]{3,2,1,0:T(8,128)}, f32[1,3,8,512]{3,2,1,0:T(8,128)}, u32[]{:S(2)}, u32[]{:S(2)}) collective-permute-start(f32[1,3,8,512]{3,2,1,0:T(8,128)} %get-tuple-element.53), channel_id=1, source_target_pairs={{0,8},{8,16},{16,24},{24,32},{32,40},{40,48},{48,56},{56,64},{64,7... | collective-permute-start | bytes 147464 | tf_op jit(solution)/shard_map/ppermute | solution.py:20
  20.0 68.6 %collective-permute-start.9 = (f32[2,32,1,128]{3,1,2,0:T(8,128)}, f32[2,32,1,128]{3,1,2,0:T(8,128)}, u32[]{:S(2)}, u32[]{:S(2)}) collective-permute-start(f32[2,32,1,128]{3,1,2,0:T(8,128)} %bitcast.50), channel_id=1, source_target_pairs={{8,0},{16,8},{24,16},{32,24},{40,32},{48,40},{56,48},{64,56},{72,6... | collective-permute-start | bytes 98312 | tf_op jit(solution)/shard_map/ppermute | solution.py:21
  28.7 22.5 %collective-permute-start.8 = (f32[32,1,128]{2,0,1:T(8,128)}, f32[32,1,128]{2,0,1:T(8,128)S(1)}, u32[]{:S(2)}, u32[]{:S(2)}) collective-permute-start(f32[32,1,128]{2,0,1:T(8,128)} %get-tuple-element.47), channel_id=1, source_target_pairs={{8,0},{16,8},{24,16},{32,24},{40,32},{48,40},{56,48},{64,56},{72,6... | collective-permute-start | bytes 49160 | tf_op jit(solution)/shard_map/ppermute | solution.py:21
  30.6 20.6 %collective-permute-start.10 = (f32[32,1,128]{2,0,1:T(8,128)}, f32[32,1,128]{2,0,1:T(8,128)S(1)}, u32[]{:S(2)}, u32[]{:S(2)}) collective-permute-start(f32[32,1,128]{2,0,1:T(8,128)} %get-tuple-element.46), channel_id=1, source_target_pairs={{0,8},{8,16},{16,24},{24,32},{32,40},{40,48},{48,56},{56,64},{64,7... | collective-permute-start | bytes 49160 | tf_op jit(solution)/shard_map/ppermute | solution.py:20
  54.2 11.0 %collective-permute-start.12 = (f32[32,66,1]{1,0,2:T(8,128)}, f32[32,66,1]{1,0,2:T(8,128)S(1)}, u32[]{:S(2)}, u32[]{:S(2)}) collective-permute-start(f32[32,66,1]{1,0,2:T(8,128)} %copy.134), channel_id=1, source_target_pairs={{1,0},{2,1},{3,2},{4,3},{5,4},{6,5},{7,6},{9,8},{10,9},{11,10},{12... | collective-permute-start | bytes 25352 | tf_op jit(solution)/shard_map/ppermute | solution.py:21
  58.9 9.8 %collective-permute-start.14 = (f32[32,66,1]{1,0,2:T(8,128)S(1)}, f32[32,66,1]{1,0,2:T(8,128)}, u32[]{:S(2)}, u32[]{:S(2)}) collective-permute-start(f32[32,66,1]{1,0,2:T(8,128)S(1)} %copy.141), channel_id=1, source_target_pairs={{0,1},{1,2},{2,3},{3,4},{4,5},{5,6},{6,7},{8,9},{9,10},{10,11},{11... | collective-permute-start | bytes 25352 | tf_op jit(solution)/shard_map/ppermute | solution.py:20
  65.3 28.4 %collective-permute-start.11 = (f32[2,32,1,128]{3,1,2,0:T(8,128)}, f32[2,32,1,128]{3,1,2,0:T(8,128)S(1)}, u32[]{:S(2)}, u32[]{:S(2)}) collective-permute-start(f32[2,32,1,128]{3,1,2,0:T(8,128)} %bitcast.117), channel_id=1, source_target_pairs={{0,8},{8,16},{16,24},{24,32},{32,40},{40,48},{48,56},{56,64},{64,7... | collective-permute-start | bytes 98312 | tf_op jit(solution)/shard_map/ppermute | solution.py:20
  99.2 11.0 %collective-permute-start.15 = (f32[2,32,66,1]{2,1,3,0:T(8,128)S(1)}, f32[2,32,66,1]{2,1,3,0:T(8,128)S(1)}, u32[]{:S(2)}, u32[]{:S(2)}) collective-permute-start(f32[2,32,66,1]{2,1,3,0:T(8,128)S(1)} %get-tuple-element.21), channel_id=1, source_target_pairs={{0,1},{1,2},{2,3},{3,4},{4,5},{5,6},{6,7},{8,9},{9,10},{10,11},{11... | collective-permute-start | bytes 50696 | tf_op jit(solution)/shard_map/ppermute | solution.py:20
  101.7 8.5 %collective-permute-start.13 = (f32[2,32,66,1]{2,1,3,0:T(8,128)S(1)}, f32[2,32,66,1]{2,1,3,0:T(8,128)S(1)}, u32[]{:S(2)}, u32[]{:S(2)}) collective-permute-start(f32[2,32,66,1]{2,1,3,0:T(8,128)S(1)} %get-tuple-element.20), channel_id=1, source_target_pairs={{1,0},{2,1},{3,2},{4,3},{5,4},{6,5},{7,6},{9,8},{10,9},{11,10},{12... | collective-permute-start | bytes 50696 | tf_op jit(solution)/shard_map/ppermute | solution.py:21
  104.4 29.0 %collective-permute-start.3 = (f32[5,1,8,512]{3,2,1,0:T(8,128)S(1)}, f32[5,1,8,512]{3,2,1,0:T(8,128)S(1)}, u32[]{:S(2)}, u32[]{:S(2)}) collective-permute-start(f32[5,1,8,512]{3,2,1,0:T(8,128)S(1)} %get-tuple-element.52), channel_id=1, source_target_pairs={{1,0},{2,1},{3,2},{4,3},{5,4},{6,5},{7,6},{9,8},{10,9},{11,10},{12... | collective-permute-start | bytes 245768 | tf_op jit(solution)/shard_map/ppermute | solution.py:21
  106.9 26.6 %collective-permute-start.2 = (f32[5,1,8,512]{3,2,1,0:T(8,128)S(1)}, f32[5,1,8,512]{3,2,1,0:T(8,128)S(1)}, u32[]{:S(2)}, u32[]{:S(2)}) collective-permute-start(f32[5,1,8,512]{3,2,1,0:T(8,128)S(1)} %get-tuple-element.51), channel_id=1, source_target_pairs={{0,1},{1,2},{2,3},{3,4},{4,5},{5,6},{6,7},{8,9},{9,10},{10,11},{11... | collective-permute-start | bytes 245768 | tf_op jit(solution)/shard_map/ppermute | solution.py:20
  469.5 36.3 %collective-permute-start.5 = (f32[1,3,4,512]{3,2,1,0:T(4,128)S(1)}, f32[1,3,4,512]{3,2,1,0:T(4,128)S(1)}, u32[]{:S(2)}, u32[]{:S(2)}) collective-permute-start(f32[1,3,4,512]{3,2,1,0:T(4,128)S(1)} %reverse_bitcast_fusion), channel_id=1, source_target_pairs={{8,0},{16,8},{24,16},{32,24},{40,32},{48,40},{56,48},{64,56},{72,6... | collective-permute-start | bytes 73736 | tf_op jit(solution)/shard_map/ppermute | solution.py:21
  479.0 11.0 %collective-permute-start.16 = (f32[2,32,1,128]{3,1,2,0:T(8,128)S(1)}, f32[2,32,1,128]{3,1,2,0:T(8,128)S(1)}, u32[]{:S(2)}, u32[]{:S(2)}) collective-permute-start(f32[2,32,1,128]{3,1,2,0:T(8,128)S(1)} %copy.153), channel_id=1, source_target_pairs={{8,0},{16,8},{24,16},{32,24},{40,32},{48,40},{56,48},{64,56},{72,6... | collective-permute-start | bytes 98312 | tf_op jit(solution)/shard_map/ppermute | solution.py:21
  484.6 10.3 %collective-permute-start.17 = (f32[2,32,1,128]{3,1,2,0:T(8,128)S(1)}, f32[2,32,1,128]{3,1,2,0:T(8,128)S(1)}, u32[]{:S(2)}, u32[]{:S(2)}) collective-permute-start(f32[2,32,1,128]{3,1,2,0:T(8,128)S(1)} %copy.155), channel_id=1, source_target_pairs={{0,8},{8,16},{16,24},{24,32},{32,40},{40,48},{48,56},{56,64},{64,7... | collective-permute-start | bytes 98312 | tf_op jit(solution)/shard_map/ppermute | solution.py:20
  488.0 17.8 %collective-permute-start.4 = (f32[1,3,4,512]{3,2,1,0:T(4,128)S(1)}, f32[1,3,4,512]{3,2,1,0:T(4,128)S(1)}, u32[]{:S(2)}, u32[]{:S(2)}) collective-permute-start(f32[1,3,4,512]{3,2,1,0:T(4,128)S(1)} %reverse_bitcast_fusion.1), channel_id=1, source_target_pairs={{0,8},{8,16},{16,24},{24,32},{32,40},{40,48},{48,56},{56,64},{64,7... | collective-permute-start | bytes 73736 | tf_op jit(solution)/shard_map/ppermute | solution.py:20
  500.4 11.1 %collective-permute-start.19 = (f32[2,32,66,1]{2,1,3,0:T(8,128)S(1)}, f32[2,32,66,1]{2,1,3,0:T(8,128)S(1)}, u32[]{:S(2)}, u32[]{:S(2)}) collective-permute-start(f32[2,32,66,1]{2,1,3,0:T(8,128)S(1)} %get-tuple-element.19), channel_id=1, source_target_pairs={{0,1},{1,2},{2,3},{3,4},{4,5},{5,6},{6,7},{8,9},{9,10},{10,11},{11... | collective-permute-start | bytes 50696 | tf_op jit(solution)/shard_map/ppermute | solution.py:20
  505.9 68.6 %collective-permute-start.7 = (f32[5,1,4,512]{3,2,1,0:T(4,128)S(1)}, f32[5,1,4,512]{3,2,1,0:T(4,128)S(1)}, u32[]{:S(2)}, u32[]{:S(2)}) collective-permute-start(f32[5,1,4,512]{3,2,1,0:T(4,128)S(1)} %get-tuple-element.73), channel_id=1, source_target_pairs={{1,0},{2,1},{3,2},{4,3},{5,4},{6,5},{7,6},{9,8},{10,9},{11,10},{12... | collective-permute-start | bytes 122888 | tf_op jit(solution)/shard_map/ppermute | solution.py:21
  508.4 66.1 %collective-permute-start.6 = (f32[5,1,4,512]{3,2,1,0:T(4,128)S(1)}, f32[5,1,4,512]{3,2,1,0:T(4,128)S(1)}, u32[]{:S(2)}, u32[]{:S(2)}) collective-permute-start(f32[5,1,4,512]{3,2,1,0:T(4,128)S(1)} %get-tuple-element.72), channel_id=1, source_target_pairs={{0,1},{1,2},{2,3},{3,4},{4,5},{5,6},{6,7},{8,9},{9,10},{10,11},{11... | collective-permute-start | bytes 122888 | tf_op jit(solution)/shard_map/ppermute | solution.py:20
  543.0 16.3 %collective-permute-start.20 = (f32[2,32,1,128]{3,1,2,0:T(8,128)S(1)}, f32[2,32,1,128]{3,1,2,0:T(8,128)S(1)}, u32[]{:S(2)}, u32[]{:S(2)}) collective-permute-start(f32[2,32,1,128]{3,1,2,0:T(8,128)S(1)} %copy.159), channel_id=1, source_target_pairs={{8,0},{16,8},{24,16},{32,24},{40,32},{48,40},{56,48},{64,56},{72,6... | collective-permute-start | bytes 98312 | tf_op jit(solution)/shard_map/ppermute | solution.py:21
  552.4 11.5 %collective-permute-start.21 = (f32[2,32,1,128]{3,1,2,0:T(8,128)S(1)}, f32[2,32,1,128]{3,1,2,0:T(8,128)S(1)}, u32[]{:S(2)}, u32[]{:S(2)}) collective-permute-start(f32[2,32,1,128]{3,1,2,0:T(8,128)S(1)} %copy.161), channel_id=1, source_target_pairs={{0,8},{8,16},{16,24},{24,32},{32,40},{40,48},{48,56},{56,64},{64,7... | collective-permute-start | bytes 98312 | tf_op jit(solution)/shard_map/ppermute | solution.py:20
  610.3 40.9 %collective-permute-start.24 = (f32[2,32,1,128]{3,1,2,0:T(8,128)S(1)}, f32[2,32,1,128]{3,1,2,0:T(8,128)S(1)}, u32[]{:S(2)}, u32[]{:S(2)}) collective-permute-start(f32[2,32,1,128]{3,1,2,0:T(8,128)S(1)} %copy.165), channel_id=1, source_target_pairs={{8,0},{16,8},{24,16},{32,24},{40,32},{48,40},{56,48},{64,56},{72,6... | collective-permute-start | bytes 98312 | tf_op jit(solution)/shard_map/ppermute | solution.py:21
  620.3 35.4 %collective-permute-start.25 = (f32[2,32,1,128]{3,1,2,0:T(8,128)}, f32[2,32,1,128]{3,1,2,0:T(8,128)}, u32[]{:S(2)}, u32[]{:S(2)}) collective-permute-start(f32[2,32,1,128]{3,1,2,0:T(8,128)} %copy.167), channel_id=1, source_target_pairs={{0,8},{8,16},{16,24},{24,32},{32,40},{40,48},{48,56},{56,64},{64,7... | collective-permute-start | bytes 98312 | tf_op jit(solution)/shard_map/ppermute | solution.py:20
  662.0 7.7 %collective-permute-start.27 = (f32[2,32,66,1]{2,1,3,0:T(8,128)S(1)}, f32[2,32,66,1]{2,1,3,0:T(8,128)S(1)}, u32[]{:S(2)}, u32[]{:S(2)}) collective-permute-start(f32[2,32,66,1]{2,1,3,0:T(8,128)S(1)} %get-tuple-element.15), channel_id=1, source_target_pairs={{0,1},{1,2},{2,3},{3,4},{4,5},{5,6},{6,7},{8,9},{9,10},{10,11},{11... | collective-permute-start | bytes 50696 | tf_op jit(solution)/shard_map/ppermute | solution.py:20
  (40 other events, 699.8 us)
where the time goes:
time: 710 us; the launch traced here: 701 us
  other arithmetic  334 us (47%)
  local copies, waits for them, and re-layouts  276 us (39%)
  starting transfers between devices  85.5 us (12%)
    scatter-add x4, other arithmetic, per_device(): contrib = contrib.at[:, remap_slot[k]].add(remap_weight[k] * flux)  175 us
    gather x8, local copies, waits for them, and re-layouts, per_device(): remapped = remapped + remap_weight[k] * received[:, remap_slot[k]]  130 us
    add x4, other arithmetic, update(): center + lap  74.9 us
    ppermute x14, starting transfers between devices, padded_2(): after = lax.ppermute(first, axis, down)  47.9 us
    ppermute x14, starting transfers between devices, padded_2(): before = lax.ppermute(last, axis, up)  37.5 us
    concatenate x7, other arithmetic, update(): return jnp.concatenate([fresh[:, :1] + forcing[:, None], fresh[:, 1:]], 1)  29.9 us
    scatter-add x1, other arithmetic, per_device(): jnp.zeros((nflux, ncols), jnp.float32).at[:, columns].add(returned)  25.8 us
    ppermute x5, local copies, waits for them, and re-layouts, padded_2(): before = lax.ppermute(last, axis, up)  20.3 us
  transfers between devices with their start and end apart: 28, of which 2 were waited for; matrix products, arithmetic and copies ran while one was open for 27% of the time, Pallas kernels for 0%

commit v1 on v0

v1 whole, which is shorter than its diff:
```python
import functools

import jax
import jax.numpy as jnp
from jax import lax
from jax.experimental import pallas as pl
from jax.experimental.pallas import tpu as pltpu
from jax.sharding import PartitionSpec as P

MESH = pl.DeviceIdType.MESH
F32, BF16, I32 = jnp.float32, jnp.bfloat16, jnp.int32
NFIELD, AC, SLOT, K, CX, CY, LEV, STEPS = 8, 2048, 512, 4, 64, 128, 32, 4
OFFSETS = [(o // 3 - 1, o % 3 - 1) for o in range(9)]
AROUND = [o for o in range(9) if o != 4]
XT = CX // 8
GROUPS = LEV // 4
PAD = CX + 16


def lanes(shape):
    return lax.broadcasted_iota(I32, shape, len(shape) - 1)


def rows(shape):
    return lax.broadcasted_iota(I32, shape, len(shape) - 2)


def split_pair(v):
    head = v.astype(BF16).astype(F32)
    return jnp.where(rows(v.shape) < 4, head, v - head)


def onehot_rows(index, count):
    return jnp.where(rows((count, 128)) == index, 1.0, 0.0).astype(BF16)


def spread(pair, high, count):
    parts = [jnp.where(high == h, pair, 0.0) for h in range(count)]
    return jnp.concatenate(parts, 0).astype(BF16)


def kernel(
    pc_ref, atm_hbm, cols_hbm, slot_hbm, weight_hbm, land_hbm, tr_hbm, kap_hbm,
    flux_hbm, out_hbm,
    atm, cols, slot, weight, land, tr, kap, aflux,
    psend, precv, bsend, bret, remap, flux8, force,
    s_ref, a_ref, b_ref, c_one, c_two, c_out, u_one, u_two, comb,
    spread_s, onehot_s,
    xsend, xrecv, ysend, yrecv, sxsend, sxrecv, sysend, syrecv,
    in_sem, out_sem, ps_sem, pr_sem, bs_sem, br_sem, hs_sem, hr_sem,
):
    gx, gy = lax.axis_index("gx"), lax.axis_index("gy")
    n_gx, n_gy = lax.axis_size("gx"), lax.axis_size("gy")

    def inside(dx, dy):
        ok = None
        for at, d, n in ((gx, dx, n_gx), (gy, dy, n_gy)):
            c = at > 0 if d < 0 else at < n - 1 if d > 0 else None
            if c is not None:
                ok = c if ok is None else ok & c
        return ok

    sources = (atm_hbm, cols_hbm, slot_hbm, weight_hbm, land_hbm, tr_hbm, kap_hbm)
    targets = (atm, cols, slot, weight, land, tr, kap)
    loads = [pltpu.make_async_copy(a, b, in_sem.at[i]) for i, (a, b) in enumerate(zip(sources, targets))]
    for i in (0, 1, 4, 6, 5, 2, 3):
        loads[i].start()

    barrier = pltpu.get_barrier_semaphore()
    for o in AROUND:
        dx, dy = OFFSETS[o]

        @pl.when(inside(dx, dy))
        def _():
            pl.semaphore_signal(barrier, inc=1, device_id=(gx + dx, gy + dy), device_id_type=MESH)

    for side, missing in ((0, gx == 0), (1, gx == n_gx - 1)):
        @pl.when(missing)
        def _():
            for step in range(STEPS):
                xrecv[step, side] = jnp.zeros((2 * LEV, CY), F32)
            sxrecv[side] = jnp.zeros((LEV, CY), F32)
    for side, missing in ((0, gy == 0), (1, gy == n_gy - 1)):
        @pl.when(missing)
        def _():
            for step in range(STEPS):
                yrecv[step, side] = jnp.zeros((GROUPS, 8, 128), F32)
            syrecv[side] = jnp.zeros((LEV // 8, 8, 128), F32)

    def live(o, base, width):
        count = jnp.broadcast_to(pc_ref[0:1, o:o + 1], (8, width))
        return lanes((8, width)) + base < count

    loads[0].wait()
    loads[1].wait()
    for o in range(9):
        for q in range(SLOT // 128):
            index = jnp.broadcast_to(cols[0, o:o + 1, q * 128:q * 128 + 128], (8, 128))
            low, high = index & 127, index >> 7
            r = jnp.zeros((8, 128), F32)
            for h in range(AC // 128):
                got = jnp.take_along_axis(atm[:, h * 128:h * 128 + 128], low, axis=1, mode="promise_in_bounds")
                r = jnp.where(high == h, got, r)
            r = jnp.where(live(o, q * 128, 128), r, 0.0)
            if o == 4:
                precv[o, :, q * 128:q * 128 + 128] = r
            else:
                psend[o, :, q * 128:q * 128 + 128] = r

    loads[4].wait()
    loads[6].wait()
    loads[5].wait()
    lane = lanes((8, 128))

    def edge(acc, v, i):
        turned = pltpu.roll(v, 2 * i + 1, 1)
        return jnp.where((lane == 2 * i) | (lane == 2 * i + 1), turned, acc)

    def start_s(g, c):
        acc = jnp.zeros((8, 128), F32)
        for dl in range(8):
            lev = g * 8 + dl
            for xt in range(XT):
                at = slice(xt * 8, xt * 8 + 8)
                wet = land[at, :].astype(F32)
                v = jnp.sqrt(kap[lev, at, :] * wet)
                s_ref[pl.ds(pl.multiple_of(lev * PAD + 8 + xt * 8, 8), 8), :] = v
                acc = edge(acc, v, dl * 8 + xt)
        sysend[g] = acc
        return c

    lax.fori_loop(0, LEV // 8, start_s, 0)

    def start_u(g, c):
        acc = jnp.zeros((8, 128), F32)
        for dl in range(4):
            lev = g * 4 + dl
            for xt in range(XT):
                s = s_ref[pl.ds(pl.multiple_of(lev * PAD + 8 + xt * 8, 8), 8), :]
                for t in range(2):
                    u = s * tr[t, lev, xt * 8:xt * 8 + 8, :]
                    u_one[pl.ds(pl.multiple_of((t * LEV + lev) * PAD + 8 + xt * 8, 8), 8), :] = u
                    acc = edge(acc, u, dl * 16 + t * 8 + xt)
        ysend[0, g] = acc
        return c

    lax.fori_loop(0, GROUPS, start_u, 0)

    for xt in range(XT):
        at = slice(xt * 8, xt * 8 + 8)
        b_ref[at, :] = 0.05 * land[at, :].astype(F32)

    def edge_rows(src, dst, levels):
        for j in range(levels // 8):
            dst[0, j * 8:j * 8 + 8, :] = src[pl.ds(j * 8 * PAD + 8 + CX - 1, 8, stride=PAD), :]
            dst[1, j * 8:j * 8 + 8, :] = src[pl.ds(j * 8 * PAD + 8, 8, stride=PAD), :]

    def halo_rows(src, dst, levels):
        for j in range(levels // 8):
            dst[pl.ds(j * 8 * PAD + 7, 8, stride=PAD), :] = src[0, j * 8:j * 8 + 8, :]
            dst[pl.ds(j * 8 * PAD + 8 + CX, 8, stride=PAD), :] = src[1, j * 8:j * 8 + 8, :]

    def halo_copies(xs, xr, ys, yr, n):
        made = []
        for side, (dx, dy) in enumerate(((1, 0), (-1, 0), (0, 1), (0, -1))):
            src = xs.at[side] if side < 2 else ys
            dst = xr.at[side] if side < 2 else yr.at[side - 2]
            copy = pltpu.make_async_remote_copy(
                src_ref=src, dst_ref=dst, send_sem=hs_sem.at[n, side], recv_sem=hr_sem.at[n, side],
                device_id=(gx + dx, gy + dy), device_id_type=MESH)
            made.append((inside(dx, dy), inside(-dx, -dy), copy))
        return made

    def offset_copies(src, dst, ss, rs, sign):
        made = []
        for o in AROUND:
            dx, dy = OFFSETS[o][0] * sign, OFFSETS[o][1] * sign
            copy = pltpu.make_async_remote_copy(
                src_ref=src.at[o], dst_ref=dst.at[o], send_sem=ss.at[o], recv_sem=rs.at[o],
                device_id=(gx + dx, gy + dy), device_id_type=MESH)
            made.append((inside(dx, dy), inside(-dx, -dy), copy))
        return made

    def start(copies):
        for can, _, copy in copies:
            pl.when(can)(copy.start)

    def received(copies):
        for _, comes, copy in copies:
            pl.when(comes)(copy.wait_recv)

    def sent(copies):
        for can, _, copy in copies:
            pl.when(can)(copy.wait_send)

    wide = 1 + (gx > 0).astype(I32) + (gx < n_gx - 1).astype(I32)
    high = 1 + (gy > 0).astype(I32) + (gy < n_gy - 1).astype(I32)
    pl.semaphore_wait(barrier, wide * high - 1)

    packs = offset_copies(psend, precv, ps_sem, pr_sem, 1)
    start(packs)
    edge_rows(s_ref, sxsend, LEV)
    s_halos = halo_copies(sxsend, sxrecv, sysend, syrecv, STEPS)
    start(s_halos)
    edge_rows(u_one, xsend.at[0], 2 * LEV)
    u_halos = [halo_copies(xsend.at[n], xrecv.at[n], ysend.at[n], yrecv.at[n], n) for n in range(STEPS)]
    start(u_halos[0])

    def columns_in(src, groups):
        for g in range(groups):
            comb[g] = jnp.where(lane % 2 == 1, pltpu.roll(src[0, g], 1, 1), pltpu.roll(src[1, g], 127, 1))

    def across(u, packed, i):
        halo = pltpu.roll(packed, 127 - 2 * i, 1)
        left = jnp.where(lane == 0, halo, pltpu.roll(u, 1, 1))
        right = jnp.where(lane == 127, halo, pltpu.roll(u, 127, 1))
        return left + right

    received(s_halos)
    halo_rows(sxrecv, s_ref, LEV)
    columns_in(syrecv, LEV // 8)

    def centre(g, c):
        packed = comb[g]
        for dl in range(8):
            lev = g * 8 + dl
            for xt in range(XT):
                base = lev * PAD + 8 + xt * 8
                s = s_ref[pl.ds(pl.multiple_of(base, 8), 8), :]
                total = across(s, packed, dl * 8 + xt) + s_ref[pl.ds(base - 1, 8), :] + s_ref[pl.ds(base + 1, 8), :]
                a_ref[lev, xt * 8:xt * 8 + 8, :] = 1.0 - s * total - 2.0 * b_ref[xt * 8:xt * 8 + 8, :]
        return c

    lax.fori_loop(0, LEV // 8, centre, 0)

    loads[2].wait()
    loads[3].wait()
    received(packs)

    def gather(i, c):
        for xx in range(4):
            x = i * 4 + xx
            acc = jnp.zeros((8, 128), F32)
            for k in range(K):
                index = jnp.broadcast_to(slot[k, pl.ds(x, 1), :], (8, 128))
                low, high = index & 127, index >> 7
                r = jnp.zeros((8, 128), F32)
                for h in range(36):
                    table = precv[h // 4, :, (h % 4) * 128:(h % 4) * 128 + 128]
                    got = jnp.take_along_axis(table, low, axis=1, mode="promise_in_bounds")
                    r = jnp.where(high == h, got, r)
                acc = acc + jnp.broadcast_to(weight[k, pl.ds(x, 1), :], (8, 128)) * r
            remap[pl.ds(pl.multiple_of(x * 8, 8), 8), :] = acc
        return c

    lax.fori_loop(0, CX // 4, gather, 0)

    for xt in range(XT):
        at = slice(xt * 8, xt * 8 + 8)
        r = [remap[pl.ds(xt * 64 + f, 8, stride=8), :] for f in range(NFIELD)]
        wet = land[at, :].astype(F32)
        ws = jnp.sqrt(r[0] * r[0] + r[1] * r[1] + 1.0)
        heat = (ws * (r[2] - tr[0, 0, at, :]) + r[4] + r[5]) * wet
        water = (ws * (r[3] - 0.2 * tr[1, 0, at, :]) - r[6]) * wet
        sx = (ws * r[0] + 0.5 * r[7]) * wet
        sy = (ws * r[1] - 0.5 * r[7]) * wet
        for g, v in enumerate((heat, water, sx, sy)):
            flux8[pl.ds(xt * 64 + g, 8, stride=8), :] = v
            flux8[pl.ds(xt * 64 + g + 4, 8, stride=8), :] = v
        force[0, 0, at, :] = 0.05 * heat
        force[0, 1, at, :] = -0.05 * water
        force[1, 0, at, :] = jnp.zeros((8, CY), F32)
        force[1, 1, at, :] = jnp.zeros((8, CY), F32)

    def diffuse(step, c_src, c_dst, u_src, u_dst):
        received(u_halos[step])
        halo_rows(xrecv.at[step], u_src, 2 * LEV)
        columns_in(yrecv.at[step], GROUPS)
        last = step == STEPS - 1

        def group(g, c):
            packed = comb[g]
            acc = jnp.zeros((8, 128), F32)
            added = jnp.minimum(g, 1)
            for dl in range(4):
                lev = g * 4 + dl
                above, below = jnp.maximum(lev - 1, 0), jnp.minimum(lev + 1, LEV - 1)
                for xt in range(XT):
                    at = slice(xt * 8, xt * 8 + 8)
                    s = s_ref[pl.ds(pl.multiple_of(lev * PAD + 8 + xt * 8, 8), 8), :]
                    a, b = a_ref[lev, at, :], b_ref[at, :]
                    for t in range(2):
                        base = (t * LEV + lev) * PAD + 8 + xt * 8
                        i = dl * 16 + t * 8 + xt
                        u = u_src[pl.ds(pl.multiple_of(base, 8), 8), :]
                        total = across(u, packed, i) + u_src[pl.ds(base - 1, 8), :] + u_src[pl.ds(base + 1, 8), :]
                        new = a * c_src[t, lev, at, :] + s * total + b * (c_src[t, above, at, :] + c_src[t, below, at, :])
                        if dl == 0:
                            new = new + force[added, t, at, :]
                        c_dst[t, lev, at, :] = new
                        if not last:
                            u = s * new
                            u_dst[pl.ds(pl.multiple_of(base, 8), 8), :] = u
                            acc = edge(acc, u, i)
            if not last:
                ysend[step + 1, g] = acc
            return c

        lax.fori_loop(0, GROUPS, group, 0)
        if not last:
            edge_rows(u_dst, xsend.at[step + 1], 2 * LEV)
            start(u_halos[step + 1])

    diffuse(0, tr, c_one, u_one, u_two)

    def scatter_rows(i, c):
        for xx in range(8):
            x = i * 8 + xx
            for k in range(K):
                index = slot[k, pl.ds(x, 1), :]
                v = jnp.broadcast_to(weight[k, pl.ds(x, 1), :], (8, 128)) * flux8[pl.ds(pl.multiple_of(x * 8, 8), 8), :]
                to = slice((xx * K + k) * 128, (xx * K + k) * 128 + 128)
                onehot_s[:, to] = onehot_rows(index & 255, 256)
                spread_s[:, to] = spread(split_pair(v), jnp.broadcast_to(index >> 8, (8, 128)), 18)
        return c + lax.dot_general(
            spread_s[:, :4096], onehot_s[:, :4096], (((1,), (1,)), ((), ())), preferred_element_type=F32)

    back = lax.fori_loop(0, CX // 8, scatter_rows, jnp.zeros((144, 256), F32))
    for o in range(9):
        for half in range(2):
            h = o * 2 + half
            v = back[h * 8:h * 8 + 4] + back[h * 8 + 4:h * 8 + 8]
            if o == 4:
                bret[o, half * 4:half * 4 + 4, :] = v
            else:
                bsend[o, half * 4:half * 4 + 4, :] = v
    backs = offset_copies(bsend, bret, bs_sem, br_sem, -1)
    start(backs)

    diffuse(1, c_one, c_two, u_two, u_one)

    received(backs)
    for o in range(9):
        for q in range(4):
            half, at = q // 2, slice((q % 2) * 128, (q % 2) * 128 + 128)
            v = bret[o, :, at]
            swapped = pltpu.roll(v, 4, 0)
            first = rows((8, 128)) < 4
            v = jnp.where(first, v, swapped) if half == 0 else jnp.where(first, swapped, v)
            v = jnp.where(live(o, q * 128, 128), v, 0.0)
            index = cols[0, o:o + 1, q * 128:q * 128 + 128]
            to = slice((o * 4 + q) * 128, (o * 4 + q) * 128 + 128)
            onehot_s[:, to] = onehot_rows(index & 255, 256)
            spread_s[:64, to] = spread(split_pair(v), jnp.broadcast_to(index >> 8, (8, 128)), 8)
    cells = 36 * 128
    ends = lax.dot_general(
        spread_s[:64, :cells], onehot_s[:, :cells], (((1,), (1,)), ((), ())), preferred_element_type=F32)
    for h in range(8):
        aflux[:, h * 256:h * 256 + 256] = ends[h * 8:h * 8 + 4] + ends[h * 8 + 4:h * 8 + 8]
    flux_out = pltpu.make_async_copy(aflux, flux_hbm, out_sem.at[0])
    flux_out.start()

    diffuse(2, c_two, c_one, u_one, u_two)
    diffuse(3, c_one, c_out, u_two, u_one)
    state_out = pltpu.make_async_copy(c_out, out_hbm, out_sem.at[1])
    state_out.start()
    sent(packs)
    sent(s_halos)
    sent(backs)
    for copies in u_halos:
        sent(copies)
    flux_out.wait()
    state_out.wait()


def per_device(atm_fields, send_cols, pair_count, remap_slot, remap_weight, land_mask, tracers, kappa):
    V, S = pltpu.VMEM, pltpu.SemaphoreType
    hbm = pl.BlockSpec(memory_space=pl.ANY)
    return pl.pallas_call(
        kernel,
        out_shape=(
            jax.ShapeDtypeStruct((4, AC), F32),
            jax.ShapeDtypeStruct((2, LEV, CX, CY), F32),
        ),
        in_specs=[pl.BlockSpec(memory_space=pltpu.VMEM)] + [hbm] * 7,
        out_specs=(hbm, hbm),
        scratch_shapes=[
            V((8, AC), F32), V((1, 9, SLOT), I32), V((K, CX, CY), I32), V((K, CX, CY), F32), V((CX, CY), I32),
            V((2, LEV, CX, CY), F32), V((LEV, CX, CY), F32), V((4, AC), F32),
            V((9, 8, SLOT), F32), V((9, 8, SLOT), F32), V((9, 8, 256), F32), V((9, 8, 256), F32),
            V((CX * 8, CY), F32), V((CX * 8, CY), F32), V((2, 2, CX, CY), F32),
            V((LEV * PAD, CY), F32), V((LEV, CX, CY), F32), V((CX, CY), F32),
            V((2, LEV, CX, CY), F32), V((2, LEV, CX, CY), F32), V((2, LEV, CX, CY), F32),
            V((2 * LEV * PAD, CY), F32), V((2 * LEV * PAD, CY), F32), V((GROUPS, 8, 128), F32),
            V((144, 36 * 128), BF16), V((256, 36 * 128), BF16),
            V((STEPS, 2, 2 * LEV, CY), F32), V((STEPS, 2, 2 * LEV, CY), F32),
            V((STEPS, GROUPS, 8, 128), F32), V((STEPS, 2, GROUPS, 8, 128), F32),
            V((2, LEV, CY), F32), V((2, LEV, CY), F32), V((LEV // 8, 8, 128), F32), V((2, LEV // 8, 8, 128), F32),
            S.DMA((7,)), S.DMA((2,)), S.DMA((9,)), S.DMA((9,)), S.DMA((9,)), S.DMA((9,)),
            S.DMA((STEPS + 1, 4)), S.DMA((STEPS + 1, 4)),
        ],
        compiler_params=pltpu.CompilerParams(
            collective_id=0, has_side_effects=True, vmem_limit_bytes=56 << 20),
        name="couple",
    )(pair_count, atm_fields, send_cols, remap_slot, remap_weight, land_mask, tracers, kappa)


def solution(mesh):
    return jax.shard_map(
        per_device,
        mesh=mesh,
        in_specs=(
            P(None, ("gx", "gy")),
            P(("gx", "gy"), None, None),
            P(("gx", "gy"), None),
            P(None, "gx", "gy"),
            P(None, "gx", "gy"),
            P("gx", "gy"),
            P(None, None, "gx", "gy"),
            P(None, "gx", "gy"),
        ),
        out_specs=(P(None, ("gx", "gy")), P(None, None, "gx", "gy")),
        check_vma=False,
    )
```

time: 710 us -> 106 us (0.15); the launches traced: 701 us -> 105 us
  other arithmetic: 334 us -> 0 us
  local copies, waits for them, and re-layouts: 276 us -> 5.87 us
  Pallas kernels: 0 us -> 98.3 us
  starting transfers between devices: 85.5 us -> 0 us
    scatter-add x5 -> x0, other arithmetic: 201 us -> none  [the longest x4 175 us: per_device(): contrib = contrib.at[:, remap_slot[k]].add(remap_weight[k] * flux)]
    gather x10 -> x0, local copies, waits for them, and re-layouts: 137 us -> none  [the longest x8 130 us: per_device(): remapped = remapped + remap_weight[k] * received[:, remap_slot[k]]]
    pallas_call x0 -> x1, Pallas kernels: none -> 98.3 us  [per_device(): pl.pallas_call(kernel, out_shape=(jax.ShapeDtypeStruct((4, AC), F32), jax...]
    ppermute x28 -> x0, starting transfers between devices: 85.5 us -> none  [the longest x14 47.9 us: padded_2(): after = lax.ppermute(first, axis, down)]
    add x7 -> x0, other arithmetic: 78 us -> none  [the longest x4 74.9 us: update(): center + lap]
    slice x25 -> x0, local copies, waits for them, and re-layouts: 52.7 us -> none  [the longest x9 15.5 us: padded_2(): last = lax.slice_in_dim(shard, length - width, length, axis=dim)]
    ppermute x10 -> x0, local copies, waits for them, and re-layouts: 40.5 us -> none  [the longest x5 20.3 us: padded_2(): before = lax.ppermute(last, axis, up)]
    concatenate x10 -> x0, other arithmetic: 30.9 us -> none  [the longest x7 29.9 us: update(): return jnp.concatenate([fresh[:, :1] + forcing[:, None], fresh[:, 1:]], 1)]
  transfers between devices with their start and end apart: 28 -> 0, of which waited for: 2 -> 0; matrix products, arithmetic and copies ran while one was open for 27% -> 0% of each run, Pallas kernels for 0% -> 0%
where the time goes in v1:
time: 106 us; the launch traced here: 105 us
  Pallas kernels  98.3 us (93%)
  local copies, waits for them, and re-layouts  5.87 us (6%)
    pallas_call x1, Pallas kernels, per_device(): pl.pallas_call(kernel, out_shape=(jax.ShapeDtypeStruct((4, AC), F32), jax...  98.3 us
    unnamed x3, local copies, waits for them, and re-layouts  5.87 us

profile of v1, /device:TPU:105, one launch (start us, length us, event | category | flops | bytes accessed | tf_op | source)
XLA Modules:
  0.0 104.9 jit_solution(5505083865607023349)
XLA Ops:
  0.6 1.3 %copy.10.cols_hbm = s32[1,9,512]{2,1,0:T(8,128)} copy(s32[1,9,512]{2,0,1:T(1,128)} %param.9) | data formatting | bytes 36864 | tf_op args[1]
  2.0 98.3 %couple.1 = (f32[4,2048]{1,0:T(4,128)}, f32[2,32,64,128]{3,2,1,0:T(8,128)}) custom-call(s32[1,9]{1,0:T(1,128)} %pc_ref.1, f32[8,2048]{1,0:T(8,128)} %atm_hbm.1, s32[1,9,512]{2,1,0:T(8,128)} %copy.10.cols_hbm, s32[4,64,128]{2,1,0:T(8,128)} %slot_hbm.1, f32[4,64,128]{2,1,0:T(8,128)} %weight_hbm.1, s32[64,128]{1,0:T(8,128)} %land_hbm.1, ...), custom_call_target="tpu_custom_call" | custom-call | tf_op jit(solution)/shard_map/couple/pallas_call | solution.py:379
  100.3 1.4 %copy.13 = f32[4,2048]{1,0:T(4,128)} copy(f32[4,2048]{1,0:T(4,128)} %get-tuple-element.4) | data formatting | bytes 65536
  101.7 3.2 %copy.14 = f32[2,32,64,128]{3,2,1,0:T(8,128)} copy(f32[2,32,64,128]{3,2,1,0:T(8,128)} %get-tuple-element.5) | data formatting | bytes 4194304

commit v2 on v1

--- a/solution.py
+++ b/solution.py
@@ -14,6 +14,7 @@
 AROUND = [o for o in range(9) if o != 4]
 XT = CX // 8
 GROUPS = LEV // 4
+GX, SX = 16, 16
 PAD = CX + 16
 
 
@@ -31,23 +32,28 @@
 
 
 def onehot_rows(index, count):
-    return jnp.where(rows((count, 128)) == index, 1.0, 0.0).astype(BF16)
+    at = rows((count, 128)).astype(F32).astype(BF16)
+    low = jnp.broadcast_to(index.astype(F32), (16, 128)).astype(BF16)
+    low = jnp.concatenate([low] * (count // 16), 0)
+    return jnp.where(at == low, jnp.ones((), BF16), jnp.zeros((), BF16))
 
 
 def spread(pair, high, count):
-    parts = [jnp.where(high == h, pair, 0.0) for h in range(count)]
-    return jnp.concatenate(parts, 0).astype(BF16)
+    two = jnp.concatenate([pair, pair], 0).astype(BF16)
+    at = (jnp.broadcast_to(high, (16, 128)) - rows((16, 128)) // 8).astype(F32).astype(BF16)
+    zero = jnp.zeros((), BF16)
+    return jnp.concatenate([jnp.where(at == jnp.asarray(2 * q, BF16), two, zero) for q in range(count // 2)], 0)
 
 
 def kernel(
     pc_ref, atm_hbm, cols_hbm, slot_hbm, weight_hbm, land_hbm, tr_hbm, kap_hbm,
-    flux_hbm, out_hbm,
-    atm, cols, slot, weight, land, tr, kap, aflux,
+    aflux, c_out,
+    atm, cols, slot, weight, land, tr, kap,
     psend, precv, bsend, bret, remap, flux8, force,
-    s_ref, a_ref, b_ref, c_one, c_two, c_out, u_one, u_two, comb,
-    spread_s, onehot_s,
+    s_ref, a_ref, b_ref, c_one, c_two, u_one, u_two, comb,
+    spread_s, onehot_s, table_s,
     xsend, xrecv, ysend, yrecv, sxsend, sxrecv, sysend, syrecv,
-    in_sem, out_sem, ps_sem, pr_sem, bs_sem, br_sem, hs_sem, hr_sem,
+    in_sem, ps_sem, pr_sem, bs_sem, br_sem, hs_sem, hr_sem,
 ):
     gx, gy = lax.axis_index("gx"), lax.axis_index("gy")
     n_gx, n_gy = lax.axis_size("gx"), lax.axis_size("gy")
@@ -95,7 +101,7 @@
     loads[1].wait()
     for o in range(9):
         for q in range(SLOT // 128):
-            index = jnp.broadcast_to(cols[0, o:o + 1, q * 128:q * 128 + 128], (8, 128))
+            index = jnp.broadcast_to(cols[o, :, q * 128:q * 128 + 128], (8, 128))
             low, high = index & 127, index >> 7
             r = jnp.zeros((8, 128), F32)
             for h in range(AC // 128):
@@ -131,6 +137,17 @@
 
     lax.fori_loop(0, LEV // 8, start_s, 0)
 
+    def edge_columns(src, dst, g, c):
+        acc = jnp.zeros((8, 128), F32)
+        for dl in range(4):
+            lev = g * 4 + dl
+            for t in range(2):
+                for xt in range(XT):
+                    base = (t * LEV + lev) * PAD + 8 + xt * 8
+                    acc = edge(acc, src[pl.ds(pl.multiple_of(base, 8), 8), :], dl * 16 + t * 8 + xt)
+        dst[g] = acc
+        return c
+
     def start_u(g, c):
         acc = jnp.zeros((8, 128), F32)
         for dl in range(4):
@@ -216,6 +233,19 @@
         right = jnp.where(lane == 127, halo, pltpu.roll(u, 127, 1))
         return left + right
 
+    loads[2].wait()
+    loads[3].wait()
+
+    def onehots(i, c):
+        for xx in range(4):
+            x = i * 4 + xx
+            for k in range(K):
+                at = pl.ds(pl.multiple_of((x * K + k) * 128, 128), 128)
+                onehot_s[:, at] = onehot_rows(slot[k, pl.ds(x, 1), :] & 255, 256)
+        return c
+
+    lax.fori_loop(0, CX // 4, onehots, 0)
+
     received(s_halos)
     halo_rows(sxrecv, s_ref, LEV)
     columns_in(syrecv, LEV // 8)
@@ -233,27 +263,65 @@
 
     lax.fori_loop(0, LEV // 8, centre, 0)
 
-    loads[2].wait()
-    loads[3].wait()
+    def diffuse(step, c_src, c_dst, u_src, u_dst):
+        received(u_halos[step])
+        halo_rows(xrecv.at[step], u_src, 2 * LEV)
+        columns_in(yrecv.at[step], GROUPS)
+
+        def group(g, c):
+            packed = comb[g]
+            added = jnp.minimum(g, 1)
+            for dl in range(4):
+                lev = g * 4 + dl
+                above, below = jnp.maximum(lev - 1, 0), jnp.minimum(lev + 1, LEV - 1)
+                for xt in range(XT):
+                    at = slice(xt * 8, xt * 8 + 8)
+                    s = s_ref[pl.ds(pl.multiple_of(lev * PAD + 8 + xt * 8, 8), 8), :]
+                    a, b = a_ref[lev, at, :], b_ref[at, :]
+                    for t in range(2):
+                        base = (t * LEV + lev) * PAD + 8 + xt * 8
+                        u = u_src[pl.ds(pl.multiple_of(base, 8), 8), :]
+                        total = across(u, packed, dl * 16 + t * 8 + xt) + u_src[pl.ds(base - 1, 8), :] + u_src[pl.ds(base + 1, 8), :]
+                        new = a * c_src[t, lev, at, :] + s * total + b * (c_src[t, above, at, :] + c_src[t, below, at, :])
+                        if dl == 0 and step > 0:
+                            new = new + force[added, t, at, :]
+                        c_dst[t, lev, at, :] = new
+                        if step < STEPS - 1:
+                            u_dst[pl.ds(pl.multiple_of(base, 8), 8), :] = s * new
+            return c
+
+        lax.fori_loop(0, GROUPS, group, 0)
+
+    def send_halos(step, src):
+        lax.fori_loop(0, GROUPS, functools.partial(edge_columns, src, ysend.at[step]), 0)
+        edge_rows(src, xsend.at[step], 2 * LEV)
+        start(u_halos[step])
+
+    diffuse(0, tr, c_one, u_one, u_two)
+
     received(packs)
 
+    table = jnp.concatenate([precv[h // 2, :, (h % 2) * 256:(h % 2) * 256 + 256] for h in range(18)], 0)
+    head = table.astype(BF16)
+    table_s[0] = head
+    table_s[1] = (table - head.astype(F32)).astype(BF16)
+
     def gather(i, c):
-        for xx in range(4):
-            x = i * 4 + xx
+        for xx in range(GX):
+            x = i * GX + xx
+            hot = onehot_s[:, pl.ds(pl.multiple_of(x * K * 128, 512), K * 128)]
+            found = jnp.dot(table_s[0], hot, preferred_element_type=F32) + jnp.dot(table_s[1], hot, preferred_element_type=F32)
             acc = jnp.zeros((8, 128), F32)
             for k in range(K):
-                index = jnp.broadcast_to(slot[k, pl.ds(x, 1), :], (8, 128))
-                low, high = index & 127, index >> 7
+                high = jnp.broadcast_to(slot[k, pl.ds(x, 1), :], (8, 128)) >> 8
                 r = jnp.zeros((8, 128), F32)
-                for h in range(36):
-                    table = precv[h // 4, :, (h % 4) * 128:(h % 4) * 128 + 128]
-                    got = jnp.take_along_axis(table, low, axis=1, mode="promise_in_bounds")
-                    r = jnp.where(high == h, got, r)
+                for h in range(18):
+                    r = jnp.where(high == h, found[h * 8:h * 8 + 8, k * 128:k * 128 + 128], r)
                 acc = acc + jnp.broadcast_to(weight[k, pl.ds(x, 1), :], (8, 128)) * r
             remap[pl.ds(pl.multiple_of(x * 8, 8), 8), :] = acc
         return c
 
-    lax.fori_loop(0, CX // 4, gather, 0)
+    lax.fori_loop(0, CX // GX, gather, 0)
 
     for xt in range(XT):
         at = slice(xt * 8, xt * 8 + 8)
@@ -267,65 +335,34 @@
         for g, v in enumerate((heat, water, sx, sy)):
             flux8[pl.ds(xt * 64 + g, 8, stride=8), :] = v
             flux8[pl.ds(xt * 64 + g + 4, 8, stride=8), :] = v
-        force[0, 0, at, :] = 0.05 * heat
-        force[0, 1, at, :] = -0.05 * water
+        for t, v in enumerate((0.05 * heat, -0.05 * water)):
+            force[0, t, at, :] = v
+            v = c_one[t, 0, at, :] + v
+            c_one[t, 0, at, :] = v
+            u_two[t * LEV * PAD + 8 + xt * 8:t * LEV * PAD + 16 + xt * 8, :] = s_ref[8 + xt * 8:16 + xt * 8, :] * v
         force[1, 0, at, :] = jnp.zeros((8, CY), F32)
         force[1, 1, at, :] = jnp.zeros((8, CY), F32)
 
-    def diffuse(step, c_src, c_dst, u_src, u_dst):
-        received(u_halos[step])
-        halo_rows(xrecv.at[step], u_src, 2 * LEV)
-        columns_in(yrecv.at[step], GROUPS)
-        last = step == STEPS - 1
-
-        def group(g, c):
-            packed = comb[g]
-            acc = jnp.zeros((8, 128), F32)
-            added = jnp.minimum(g, 1)
-            for dl in range(4):
-                lev = g * 4 + dl
-                above, below = jnp.maximum(lev - 1, 0), jnp.minimum(lev + 1, LEV - 1)
-                for xt in range(XT):
-                    at = slice(xt * 8, xt * 8 + 8)
-                    s = s_ref[pl.ds(pl.multiple_of(lev * PAD + 8 + xt * 8, 8), 8), :]
-                    a, b = a_ref[lev, at, :], b_ref[at, :]
-                    for t in range(2):
-                        base = (t * LEV + lev) * PAD + 8 + xt * 8
-                        i = dl * 16 + t * 8 + xt
-                        u = u_src[pl.ds(pl.multiple_of(base, 8), 8), :]
-                        total = across(u, packed, i) + u_src[pl.ds(base - 1, 8), :] + u_src[pl.ds(base + 1, 8), :]
-                        new = a * c_src[t, lev, at, :] + s * total + b * (c_src[t, above, at, :] + c_src[t, below, at, :])
-                        if dl == 0:
-                            new = new + force[added, t, at, :]
-                        c_dst[t, lev, at, :] = new
-                        if not last:
-                            u = s * new
-                            u_dst[pl.ds(pl.multiple_of(base, 8), 8), :] = u
-                            acc = edge(acc, u, i)
-            if not last:
-                ysend[step + 1, g] = acc
-            return c
-
-        lax.fori_loop(0, GROUPS, group, 0)
-        if not last:
-            edge_rows(u_dst, xsend.at[step + 1], 2 * LEV)
-            start(u_halos[step + 1])
-
-    diffuse(0, tr, c_one, u_one, u_two)
+    send_halos(1, u_two)
 
     def scatter_rows(i, c):
-        for xx in range(8):
-            x = i * 8 + xx
+        for xx in range(SX):
+            x = i * SX + xx
             for k in range(K):
-                index = slot[k, pl.ds(x, 1), :]
                 v = jnp.broadcast_to(weight[k, pl.ds(x, 1), :], (8, 128)) * flux8[pl.ds(pl.multiple_of(x * 8, 8), 8), :]
                 to = slice((xx * K + k) * 128, (xx * K + k) * 128 + 128)
-                onehot_s[:, to] = onehot_rows(index & 255, 256)
-                spread_s[:, to] = spread(split_pair(v), jnp.broadcast_to(index >> 8, (8, 128)), 18)
+                spread_s[:, to] = spread(split_pair(v), slot[k, pl.ds(x, 1), :] >> 8, 18)
+        hot = onehot_s[:, pl.ds(pl.multiple_of(i * (SX * K * 128), 512), SX * K * 128)]
         return c + lax.dot_general(
-            spread_s[:, :4096], onehot_s[:, :4096], (((1,), (1,)), ((), ())), preferred_element_type=F32)
-
-    back = lax.fori_loop(0, CX // 8, scatter_rows, jnp.zeros((144, 256), F32))
+            spread_s[:, :SX * K * 128], hot, (((1,), (1,)), ((), ())), preferred_element_type=F32)
+
+    back = lax.fori_loop(0, 2, scatter_rows, jnp.zeros((144, 256), F32))
+    diffuse(1, c_one, c_two, u_two, u_one)
+    send_halos(2, u_one)
+    back = scatter_rows(2, back)
+    diffuse(2, c_two, c_one, u_one, u_two)
+    send_halos(3, u_two)
+    back = scatter_rows(3, back)
     for o in range(9):
         for half in range(2):
             h = o * 2 + half
@@ -337,7 +374,7 @@
     backs = offset_copies(bsend, bret, bs_sem, br_sem, -1)
     start(backs)
 
-    diffuse(1, c_one, c_two, u_two, u_one)
+    diffuse(3, c_one, c_out, u_two, u_one)
 
     received(backs)
     for o in range(9):
@@ -348,29 +385,21 @@
             first = rows((8, 128)) < 4
             v = jnp.where(first, v, swapped) if half == 0 else jnp.where(first, swapped, v)
             v = jnp.where(live(o, q * 128, 128), v, 0.0)
-            index = cols[0, o:o + 1, q * 128:q * 128 + 128]
+            index = cols[o, :, q * 128:q * 128 + 128]
             to = slice((o * 4 + q) * 128, (o * 4 + q) * 128 + 128)
             onehot_s[:, to] = onehot_rows(index & 255, 256)
-            spread_s[:64, to] = spread(split_pair(v), jnp.broadcast_to(index >> 8, (8, 128)), 8)
+            spread_s[:64, to] = spread(split_pair(v), index >> 8, 8)
     cells = 36 * 128
     ends = lax.dot_general(
         spread_s[:64, :cells], onehot_s[:, :cells], (((1,), (1,)), ((), ())), preferred_element_type=F32)
     for h in range(8):
         aflux[:, h * 256:h * 256 + 256] = ends[h * 8:h * 8 + 4] + ends[h * 8 + 4:h * 8 + 8]
-    flux_out = pltpu.make_async_copy(aflux, flux_hbm, out_sem.at[0])
-    flux_out.start()
-
-    diffuse(2, c_two, c_one, u_one, u_two)
-    diffuse(3, c_one, c_out, u_two, u_one)
-    state_out = pltpu.make_async_copy(c_out, out_hbm, out_sem.at[1])
-    state_out.start()
+
     sent(packs)
     sent(s_halos)
     sent(backs)
     for copies in u_halos:
         sent(copies)
-    flux_out.wait()
-    state_out.wait()
 
 
 def per_device(atm_fields, send_cols, pair_count, remap_slot, remap_weight, land_mask, tracers, kappa):
@@ -379,30 +408,30 @@
     return pl.pallas_call(
         kernel,
         out_shape=(
-            jax.ShapeDtypeStruct((4, AC), F32),
-            jax.ShapeDtypeStruct((2, LEV, CX, CY), F32),
+            pltpu.VMEM((4, AC), F32),
+            pltpu.VMEM((2, LEV, CX, CY), F32),
         ),
         in_specs=[pl.BlockSpec(memory_space=pltpu.VMEM)] + [hbm] * 7,
-        out_specs=(hbm, hbm),
+        out_specs=(pl.BlockSpec(memory_space=pltpu.VMEM),) * 2,
         scratch_shapes=[
-            V((8, AC), F32), V((1, 9, SLOT), I32), V((K, CX, CY), I32), V((K, CX, CY), F32), V((CX, CY), I32),
-            V((2, LEV, CX, CY), F32), V((LEV, CX, CY), F32), V((4, AC), F32),
+            V((8, AC), F32), V((9, 1, SLOT), I32), V((K, CX, CY), I32), V((K, CX, CY), F32), V((CX, CY), I32),
+            V((2, LEV, CX, CY), F32), V((LEV, CX, CY), F32),
             V((9, 8, SLOT), F32), V((9, 8, SLOT), F32), V((9, 8, 256), F32), V((9, 8, 256), F32),
             V((CX * 8, CY), F32), V((CX * 8, CY), F32), V((2, 2, CX, CY), F32),
             V((LEV * PAD, CY), F32), V((LEV, CX, CY), F32), V((CX, CY), F32),
-            V((2, LEV, CX, CY), F32), V((2, LEV, CX, CY), F32), V((2, LEV, CX, CY), F32),
+            V((2, LEV, CX, CY), F32), V((2, LEV, CX, CY), F32),
             V((2 * LEV * PAD, CY), F32), V((2 * LEV * PAD, CY), F32), V((GROUPS, 8, 128), F32),
-            V((144, 36 * 128), BF16), V((256, 36 * 128), BF16),
+            V((144, 64 * 128), BF16), V((256, CX * K * 128), BF16), V((2, 144, 256), BF16),
             V((STEPS, 2, 2 * LEV, CY), F32), V((STEPS, 2, 2 * LEV, CY), F32),
             V((STEPS, GROUPS, 8, 128), F32), V((STEPS, 2, GROUPS, 8, 128), F32),
             V((2, LEV, CY), F32), V((2, LEV, CY), F32), V((LEV // 8, 8, 128), F32), V((2, LEV // 8, 8, 128), F32),
-            S.DMA((7,)), S.DMA((2,)), S.DMA((9,)), S.DMA((9,)), S.DMA((9,)), S.DMA((9,)),
+            S.DMA((7,)), S.DMA((9,)), S.DMA((9,)), S.DMA((9,)), S.DMA((9,)),
             S.DMA((STEPS + 1, 4)), S.DMA((STEPS + 1, 4)),
         ],
         compiler_params=pltpu.CompilerParams(
-            collective_id=0, has_side_effects=True, vmem_limit_bytes=56 << 20),
+            collective_id=0, has_side_effects=True, vmem_limit_bytes=52 << 20),
         name="couple",
-    )(pair_count, atm_fields, send_cols, remap_slot, remap_weight, land_mask, tracers, kappa)
+    )(pair_count, atm_fields, send_cols.transpose(1, 0, 2), remap_slot, remap_weight, land_mask, tracers, kappa)
 
 
 def solution(mesh):

time: 106 us -> 47.8 us (0.45)
  Pallas kernels: 98.3 us -> 45.1 us
  local copies, waits for them, and re-layouts: 5.87 us -> 1.94 us
    pallas_call x1, Pallas kernels: 98.3 us -> 45.1 us  [per_device(): pl.pallas_call(kernel, out_shape=(pltpu.VMEM((4, AC), F32), pltpu.VMEM((2...]
    unnamed x3 -> x2, local copies, waits for them, and re-layouts: 5.87 us -> 1.94 us
where the time goes in v2:
time: 47.8 us; the launch traced here: 47.7 us
  Pallas kernels  45.1 us (94%)
  local copies, waits for them, and re-layouts  1.94 us (4%)
  between operations  0.64 us (1%)
    pallas_call x1, Pallas kernels, per_device(): pl.pallas_call(kernel, out_shape=(pltpu.VMEM((4, AC), F32), pltpu.VMEM((2...  45.1 us
    unnamed x2, local copies, waits for them, and re-layouts  1.94 us

profile of v2, /device:TPU:105, one launch (start us, length us, event | category | flops | bytes accessed | tf_op | source)
XLA Modules:
  0.0 47.7 jit_solution(6846979027544597338)
XLA Ops:
  0.6 45.1 %couple.1 = (f32[4,2048]{1,0:T(4,128)S(1)}, f32[2,32,64,128]{3,2,1,0:T(8,128)S(1)}) custom-call(s32[1,9]{1,0:T(1,128)} %pc_ref.1, f32[8,2048]{1,0:T(8,128)} %atm_hbm.1, s32[9,1,512]{2,1,0:T(1,128)} %bitcast.1, s32[4,64,128]{2,1,0:T(8,128)} %slot_hbm.1, f32[4,64,128]{2,1,0:T(8,128)} %weight_hbm.1, s32[64,128]{1,0:T(8,128)} %land_hbm.1, ...), custom_call_target="tpu_custom_call" | custom-call | tf_op jit(solution)/shard_map/couple/pallas_call | solution.py:408
  45.7 0.6 %copy.12 = f32[4,2048]{1,0:T(4,128)} copy(f32[4,2048]{1,0:T(4,128)S(1)} %get-tuple-element.2) | data formatting | bytes 65536
  46.3 1.3 %copy.13 = f32[2,32,64,128]{3,2,1,0:T(8,128)} copy(f32[2,32,64,128]{3,2,1,0:T(8,128)S(1)} %get-tuple-element.3) | data formatting | bytes 4194304

commit v3 on v2

--- a/solution.py
+++ b/solution.py
@@ -51,7 +51,7 @@
     atm, cols, slot, weight, land, tr, kap,
     psend, precv, bsend, bret, remap, flux8, force,
     s_ref, a_ref, b_ref, c_one, c_two, u_one, u_two, comb,
-    spread_s, onehot_s, table_s,
+    spread_s, onehot_s, table_s, beside_s,
     xsend, xrecv, ysend, yrecv, sxsend, sxrecv, sysend, syrecv,
     in_sem, ps_sem, pr_sem, bs_sem, br_sem, hs_sem, hr_sem,
 ):
@@ -227,24 +227,26 @@
         for g in range(groups):
             comb[g] = jnp.where(lane % 2 == 1, pltpu.roll(src[0, g], 1, 1), pltpu.roll(src[1, g], 127, 1))
 
-    def across(u, packed, i):
-        halo = pltpu.roll(packed, 127 - 2 * i, 1)
-        left = jnp.where(lane == 0, halo, pltpu.roll(u, 1, 1))
-        right = jnp.where(lane == 127, halo, pltpu.roll(u, 127, 1))
-        return left + right
-
     loads[2].wait()
     loads[3].wait()
 
-    def onehots(i, c):
-        for xx in range(4):
-            x = i * 4 + xx
-            for k in range(K):
-                at = pl.ds(pl.multiple_of((x * K + k) * 128, 128), 128)
-                onehot_s[:, at] = onehot_rows(slot[k, pl.ds(x, 1), :] & 255, 256)
-        return c
-
-    lax.fori_loop(0, CX // 4, onehots, 0)
+    apart = jnp.abs(lax.broadcasted_iota(I32, (128, 128), 0) - lax.broadcasted_iota(I32, (128, 128), 1))
+    near = jnp.where(apart == 1, 1.0, 0.0).astype(BF16)
+    beside_s[:128] = near
+    beside_s[128:] = near
+
+    def two_parts(v):
+        head = v.astype(BF16)
+        return jnp.concatenate([head, (v - head.astype(F32)).astype(BF16)], 1)
+
+    def beside(src, bases):
+        blocks = [two_parts(src[pl.ds(pl.multiple_of(base, 8), CX), :]) for base in bases]
+        return jnp.dot(jnp.concatenate(blocks, 0), beside_s[...], preferred_element_type=F32)
+
+    def across(inner, packed, i):
+        return inner[i * 8:i * 8 + 8] + jnp.where(at_end, pltpu.roll(packed, 127 - 2 * i, 1), 0.0)
+
+    at_end = (lane == 0) | (lane == 127)
 
     received(s_halos)
     halo_rows(sxrecv, s_ref, LEV)
@@ -252,12 +254,13 @@
 
     def centre(g, c):
         packed = comb[g]
+        inner = beside(s_ref, [(g * 8 + dl) * PAD + 8 for dl in range(8)])
         for dl in range(8):
             lev = g * 8 + dl
             for xt in range(XT):
                 base = lev * PAD + 8 + xt * 8
                 s = s_ref[pl.ds(pl.multiple_of(base, 8), 8), :]
-                total = across(s, packed, dl * 8 + xt) + s_ref[pl.ds(base - 1, 8), :] + s_ref[pl.ds(base + 1, 8), :]
+                total = across(inner, packed, dl * 8 + xt) + s_ref[pl.ds(base - 1, 8), :] + s_ref[pl.ds(base + 1, 8), :]
                 a_ref[lev, xt * 8:xt * 8 + 8, :] = 1.0 - s * total - 2.0 * b_ref[xt * 8:xt * 8 + 8, :]
         return c
 
@@ -270,6 +273,7 @@
 
         def group(g, c):
             packed = comb[g]
+            inner = beside(u_src, [(t * LEV + g * 4 + dl) * PAD + 8 for dl in range(4) for t in range(2)])
             added = jnp.minimum(g, 1)
             for dl in range(4):
                 lev = g * 4 + dl
@@ -280,8 +284,7 @@
                     a, b = a_ref[lev, at, :], b_ref[at, :]
                     for t in range(2):
                         base = (t * LEV + lev) * PAD + 8 + xt * 8
-                        u = u_src[pl.ds(pl.multiple_of(base, 8), 8), :]
-                        total = across(u, packed, dl * 16 + t * 8 + xt) + u_src[pl.ds(base - 1, 8), :] + u_src[pl.ds(base + 1, 8), :]
+                        total = across(inner, packed, dl * 16 + t * 8 + xt) + u_src[pl.ds(base - 1, 8), :] + u_src[pl.ds(base + 1, 8), :]
                         new = a * c_src[t, lev, at, :] + s * total + b * (c_src[t, above, at, :] + c_src[t, below, at, :])
                         if dl == 0 and step > 0:
                             new = new + force[added, t, at, :]
@@ -309,7 +312,7 @@
     def gather(i, c):
         for xx in range(GX):
             x = i * GX + xx
-            hot = onehot_s[:, pl.ds(pl.multiple_of(x * K * 128, 512), K * 128)]
+            hot = jnp.concatenate([onehot_rows(slot[k, pl.ds(x, 1), :] & 255, 256) for k in range(K)], 1)
             found = jnp.dot(table_s[0], hot, preferred_element_type=F32) + jnp.dot(table_s[1], hot, preferred_element_type=F32)
             acc = jnp.zeros((8, 128), F32)
             for k in range(K):
@@ -346,23 +349,24 @@
     send_halos(1, u_two)
 
     def scatter_rows(i, c):
+        hots, spreads = [], []
         for xx in range(SX):
             x = i * SX + xx
             for k in range(K):
                 v = jnp.broadcast_to(weight[k, pl.ds(x, 1), :], (8, 128)) * flux8[pl.ds(pl.multiple_of(x * 8, 8), 8), :]
-                to = slice((xx * K + k) * 128, (xx * K + k) * 128 + 128)
-                spread_s[:, to] = spread(split_pair(v), slot[k, pl.ds(x, 1), :] >> 8, 18)
-        hot = onehot_s[:, pl.ds(pl.multiple_of(i * (SX * K * 128), 512), SX * K * 128)]
+                index = slot[k, pl.ds(x, 1), :]
+                hots.append(onehot_rows(index & 255, 256))
+                spreads.append(spread(split_pair(v), index >> 8, 18))
         return c + lax.dot_general(
-            spread_s[:, :SX * K * 128], hot, (((1,), (1,)), ((), ())), preferred_element_type=F32)
-
-    back = lax.fori_loop(0, 2, scatter_rows, jnp.zeros((144, 256), F32))
+            jnp.concatenate(hots, 1), jnp.concatenate(spreads, 1), (((1,), (1,)), ((), ())), preferred_element_type=F32)
+
+    back = lax.fori_loop(0, 2, scatter_rows, jnp.zeros((256, 144), F32))
     diffuse(1, c_one, c_two, u_two, u_one)
     send_halos(2, u_one)
     back = scatter_rows(2, back)
     diffuse(2, c_two, c_one, u_one, u_two)
     send_halos(3, u_two)
-    back = scatter_rows(3, back)
+    back = scatter_rows(3, back).T
     for o in range(9):
         for half in range(2):
             h = o * 2 + half
@@ -388,10 +392,9 @@
             index = cols[o, :, q * 128:q * 128 + 128]
             to = slice((o * 4 + q) * 128, (o * 4 + q) * 128 + 128)
             onehot_s[:, to] = onehot_rows(index & 255, 256)
-            spread_s[:64, to] = spread(split_pair(v), index >> 8, 8)
-    cells = 36 * 128
+            spread_s[:, to] = spread(split_pair(v), index >> 8, 8)
     ends = lax.dot_general(
-        spread_s[:64, :cells], onehot_s[:, :cells], (((1,), (1,)), ((), ())), preferred_element_type=F32)
+        spread_s[...], onehot_s[...], (((1,), (1,)), ((), ())), preferred_element_type=F32)
     for h in range(8):
         aflux[:, h * 256:h * 256 + 256] = ends[h * 8:h * 8 + 4] + ends[h * 8 + 4:h * 8 + 8]
 
@@ -421,7 +424,7 @@
             V((LEV * PAD, CY), F32), V((LEV, CX, CY), F32), V((CX, CY), F32),
             V((2, LEV, CX, CY), F32), V((2, LEV, CX, CY), F32),
             V((2 * LEV * PAD, CY), F32), V((2 * LEV * PAD, CY), F32), V((GROUPS, 8, 128), F32),
-            V((144, 64 * 128), BF16), V((256, CX * K * 128), BF16), V((2, 144, 256), BF16),
+            V((64, 36 * 128), BF16), V((256, 36 * 128), BF16), V((2, 144, 256), BF16), V((256, 128), BF16),
             V((STEPS, 2, 2 * LEV, CY), F32), V((STEPS, 2, 2 * LEV, CY), F32),
             V((STEPS, GROUPS, 8, 128), F32), V((STEPS, 2, GROUPS, 8, 128), F32),
             V((2, LEV, CY), F32), V((2, LEV, CY), F32), V((LEV // 8, 8, 128), F32), V((2, LEV // 8, 8, 128), F32),

time: 47.8 us -> 44.9 us (0.939)
  Pallas kernels: 45.1 us -> 42.2 us
    pallas_call x1, Pallas kernels: 45.1 us -> 42.2 us  [per_device(): pl.pallas_call(kernel, out_shape=(pltpu.VMEM((4, AC), F32), pltpu.VMEM((2...]
where the time goes in v3:
time: 44.9 us; the launch traced here: 44.8 us
  Pallas kernels  42.2 us (94%)
  local copies, waits for them, and re-layouts  1.94 us (4%)
  between operations  0.64 us (1%)
    pallas_call x1, Pallas kernels, per_device(): pl.pallas_call(kernel, out_shape=(pltpu.VMEM((4, AC), F32), pltpu.VMEM((2...  42.2 us
    unnamed x2, local copies, waits for them, and re-layouts  1.94 us

profile of v3, /device:TPU:105, one launch (start us, length us, event | category | flops | bytes accessed | tf_op | source)
XLA Modules:
  0.0 44.8 jit_solution(17586835829905503542)
XLA Ops:
  0.6 42.2 %couple.1 = (f32[4,2048]{1,0:T(4,128)S(1)}, f32[2,32,64,128]{3,2,1,0:T(8,128)S(1)}) custom-call(s32[1,9]{1,0:T(1,128)} %pc_ref.1, f32[8,2048]{1,0:T(8,128)} %atm_hbm.1, s32[9,1,512]{2,1,0:T(1,128)} %bitcast.1, s32[4,64,128]{2,1,0:T(8,128)} %slot_hbm.1, f32[4,64,128]{2,1,0:T(8,128)} %weight_hbm.1, s32[64,128]{1,0:T(8,128)} %land_hbm.1, ...), custom_call_target="tpu_custom_call" | custom-call | tf_op jit(solution)/shard_map/couple/pallas_call | solution.py:411
  42.8 0.6 %copy.12 = f32[4,2048]{1,0:T(4,128)} copy(f32[4,2048]{1,0:T(4,128)S(1)} %get-tuple-element.2) | data formatting | bytes 65536
  43.5 1.3 %copy.13 = f32[2,32,64,128]{3,2,1,0:T(8,128)} copy(f32[2,32,64,128]{3,2,1,0:T(8,128)S(1)} %get-tuple-element.3) | data formatting | bytes 4194304

commit v4 on v3

--- a/solution.py
+++ b/solution.py
@@ -113,9 +113,57 @@
             else:
                 psend[o, :, q * 128:q * 128 + 128] = r
 
+    def edge_rows(src, dst, levels):
+        for j in range(levels // 8):
+            dst[0, j * 8:j * 8 + 8, :] = src[pl.ds(j * 8 * PAD + 8 + CX - 1, 8, stride=PAD), :]
+            dst[1, j * 8:j * 8 + 8, :] = src[pl.ds(j * 8 * PAD + 8, 8, stride=PAD), :]
+
+    def halo_rows(src, dst, levels):
+        for j in range(levels // 8):
+            dst[pl.ds(j * 8 * PAD + 7, 8, stride=PAD), :] = src[0, j * 8:j * 8 + 8, :]
+            dst[pl.ds(j * 8 * PAD + 8 + CX, 8, stride=PAD), :] = src[1, j * 8:j * 8 + 8, :]
+
+    def halo_copies(xs, xr, ys, yr, n):
+        made = []
+        for side, (dx, dy) in enumerate(((1, 0), (-1, 0), (0, 1), (0, -1))):
+            src = xs.at[side] if side < 2 else ys
+            dst = xr.at[side] if side < 2 else yr.at[side - 2]
+            copy = pltpu.make_async_remote_copy(
+                src_ref=src, dst_ref=dst, send_sem=hs_sem.at[n, side], recv_sem=hr_sem.at[n, side],
+                device_id=(gx + dx, gy + dy), device_id_type=MESH)
+            made.append((inside(dx, dy), inside(-dx, -dy), copy))
+        return made
+
+    def offset_copies(src, dst, ss, rs, sign):
+        made = []
+        for o in AROUND:
+            dx, dy = OFFSETS[o][0] * sign, OFFSETS[o][1] * sign
+            copy = pltpu.make_async_remote_copy(
+                src_ref=src.at[o], dst_ref=dst.at[o], send_sem=ss.at[o], recv_sem=rs.at[o],
+                device_id=(gx + dx, gy + dy), device_id_type=MESH)
+            made.append((inside(dx, dy), inside(-dx, -dy), copy))
+        return made
+
+    def start(copies):
+        for can, _, copy in copies:
+            pl.when(can)(copy.start)
+
+    def received(copies):
+        for _, comes, copy in copies:
+            pl.when(comes)(copy.wait_recv)
+
+    def sent(copies):
+        for can, _, copy in copies:
+            pl.when(can)(copy.wait_send)
+
+    wide = 1 + (gx > 0).astype(I32) + (gx < n_gx - 1).astype(I32)
+    high = 1 + (gy > 0).astype(I32) + (gy < n_gy - 1).astype(I32)
+    pl.semaphore_wait(barrier, wide * high - 1)
+
+    packs = offset_copies(psend, precv, ps_sem, pr_sem, 1)
+    start(packs)
     loads[4].wait()
     loads[6].wait()
-    loads[5].wait()
     lane = lanes((8, 128))
 
     def edge(acc, v, i):
@@ -136,6 +184,9 @@
         return c
 
     lax.fori_loop(0, LEV // 8, start_s, 0)
+    edge_rows(s_ref, sxsend, LEV)
+    s_halos = halo_copies(sxsend, sxrecv, sysend, syrecv, STEPS)
+    start(s_halos)
 
     def edge_columns(src, dst, g, c):
         acc = jnp.zeros((8, 128), F32)
@@ -161,64 +212,9 @@
         ysend[0, g] = acc
         return c
 
+    loads[5].wait()
     lax.fori_loop(0, GROUPS, start_u, 0)
 
-    for xt in range(XT):
-        at = slice(xt * 8, xt * 8 + 8)
-        b_ref[at, :] = 0.05 * land[at, :].astype(F32)
-
-    def edge_rows(src, dst, levels):
-        for j in range(levels // 8):
-            dst[0, j * 8:j * 8 + 8, :] = src[pl.ds(j * 8 * PAD + 8 + CX - 1, 8, stride=PAD), :]
-            dst[1, j * 8:j * 8 + 8, :] = src[pl.ds(j * 8 * PAD + 8, 8, stride=PAD), :]
-
-    def halo_rows(src, dst, levels):
-        for j in range(levels // 8):
-            dst[pl.ds(j * 8 * PAD + 7, 8, stride=PAD), :] = src[0, j * 8:j * 8 + 8, :]
-            dst[pl.ds(j * 8 * PAD + 8 + CX, 8, stride=PAD), :] = src[1, j * 8:j * 8 + 8, :]
-
-    def halo_copies(xs, xr, ys, yr, n):
-        made = []
-        for side, (dx, dy) in enumerate(((1, 0), (-1, 0), (0, 1), (0, -1))):
-            src = xs.at[side] if side < 2 else ys
-            dst = xr.at[side] if side < 2 else yr.at[side - 2]
-            copy = pltpu.make_async_remote_copy(
-                src_ref=src, dst_ref=dst, send_sem=hs_sem.at[n, side], recv_sem=hr_sem.at[n, side],
-                device_id=(gx + dx, gy + dy), device_id_type=MESH)
-            made.append((inside(dx, dy), inside(-dx, -dy), copy))
-        return made
-
-    def offset_copies(src, dst, ss, rs, sign):
-        made = []
-        for o in AROUND:
-            dx, dy = OFFSETS[o][0] * sign, OFFSETS[o][1] * sign
-            copy = pltpu.make_async_remote_copy(
-                src_ref=src.at[o], dst_ref=dst.at[o], send_sem=ss.at[o], recv_sem=rs.at[o],
-                device_id=(gx + dx, gy + dy), device_id_type=MESH)
-            made.append((inside(dx, dy), inside(-dx, -dy), copy))
-        return made
-
-    def start(copies):
-        for can, _, copy in copies:
-            pl.when(can)(copy.start)
-
-    def received(copies):
-        for _, comes, copy in copies:
-            pl.when(comes)(copy.wait_recv)
-
-    def sent(copies):
-        for can, _, copy in copies:
-            pl.when(can)(copy.wait_send)
-
-    wide = 1 + (gx > 0).astype(I32) + (gx < n_gx - 1).astype(I32)
-    high = 1 + (gy > 0).astype(I32) + (gy < n_gy - 1).astype(I32)
-    pl.semaphore_wait(barrier, wide * high - 1)
-
-    packs = offset_copies(psend, precv, ps_sem, pr_sem, 1)
-    start(packs)
-    edge_rows(s_ref, sxsend, LEV)
-    s_halos = halo_copies(sxsend, sxrecv, sysend, syrecv, STEPS)
-    start(s_halos)
     edge_rows(u_one, xsend.at[0], 2 * LEV)
     u_halos = [halo_copies(xsend.at[n], xrecv.at[n], ysend.at[n], yrecv.at[n], n) for n in range(STEPS)]
     start(u_halos[0])
@@ -226,9 +222,6 @@
     def columns_in(src, groups):
         for g in range(groups):
             comb[g] = jnp.where(lane % 2 == 1, pltpu.roll(src[0, g], 1, 1), pltpu.roll(src[1, g], 127, 1))
-
-    loads[2].wait()
-    loads[3].wait()
 
     apart = jnp.abs(lax.broadcasted_iota(I32, (128, 128), 0) - lax.broadcasted_iota(I32, (128, 128), 1))
     near = jnp.where(apart == 1, 1.0, 0.0).astype(BF16)
@@ -247,24 +240,6 @@
         return inner[i * 8:i * 8 + 8] + jnp.where(at_end, pltpu.roll(packed, 127 - 2 * i, 1), 0.0)
 
     at_end = (lane == 0) | (lane == 127)
-
-    received(s_halos)
-    halo_rows(sxrecv, s_ref, LEV)
-    columns_in(syrecv, LEV // 8)
-
-    def centre(g, c):
-        packed = comb[g]
-        inner = beside(s_ref, [(g * 8 + dl) * PAD + 8 for dl in range(8)])
-        for dl in range(8):
-            lev = g * 8 + dl
-            for xt in range(XT):
-                base = lev * PAD + 8 + xt * 8
-                s = s_ref[pl.ds(pl.multiple_of(base, 8), 8), :]
-                total = across(inner, packed, dl * 8 + xt) + s_ref[pl.ds(base - 1, 8), :] + s_ref[pl.ds(base + 1, 8), :]
-                a_ref[lev, xt * 8:xt * 8 + 8, :] = 1.0 - s * total - 2.0 * b_ref[xt * 8:xt * 8 + 8, :]
-        return c
-
-    lax.fori_loop(0, LEV // 8, centre, 0)
 
     def diffuse(step, c_src, c_dst, u_src, u_dst):
         received(u_halos[step])
@@ -286,7 +261,7 @@
                         base = (t * LEV + lev) * PAD + 8 + xt * 8
                         total = across(inner, packed, dl * 16 + t * 8 + xt) + u_src[pl.ds(base - 1, 8), :] + u_src[pl.ds(base + 1, 8), :]
                         new = a * c_src[t, lev, at, :] + s * total + b * (c_src[t, above, at, :] + c_src[t, below, at, :])
-                        if dl == 0 and step > 0:
+                        if dl == 0:
                             new = new + force[added, t, at, :]
                         c_dst[t, lev, at, :] = new
                         if step < STEPS - 1:
@@ -300,7 +275,17 @@
         edge_rows(src, xsend.at[step], 2 * LEV)
         start(u_halos[step])
 
-    diffuse(0, tr, c_one, u_one, u_two)
+    for xt in range(XT):
+        at = slice(xt * 8, xt * 8 + 8)
+        b_ref[at, :] = 0.05 * land[at, :].astype(F32)
+
+    for o in range(9):
+        for q in range(SLOT // 128):
+            to = slice((o * 4 + q) * 128, (o * 4 + q) * 128 + 128)
+            onehot_s[:, to] = onehot_rows(cols[o, :, q * 128:q * 128 + 128] & 255, 256)
+
+    loads[2].wait()
+    loads[3].wait()
 
     received(packs)
 
@@ -338,14 +323,30 @@
         for g, v in enumerate((heat, water, sx, sy)):
             flux8[pl.ds(xt * 64 + g, 8, stride=8), :] = v
             flux8[pl.ds(xt * 64 + g + 4, 8, stride=8), :] = v
-        for t, v in enumerate((0.05 * heat, -0.05 * water)):
-            force[0, t, at, :] = v
-            v = c_one[t, 0, at, :] + v
-            c_one[t, 0, at, :] = v
-            u_two[t * LEV * PAD + 8 + xt * 8:t * LEV * PAD + 16 + xt * 8, :] = s_ref[8 + xt * 8:16 + xt * 8, :] * v
+        force[0, 0, at, :] = 0.05 * heat
+        force[0, 1, at, :] = -0.05 * water
         force[1, 0, at, :] = jnp.zeros((8, CY), F32)
         force[1, 1, at, :] = jnp.zeros((8, CY), F32)
 
+    received(s_halos)
+    halo_rows(sxrecv, s_ref, LEV)
+    columns_in(syrecv, LEV // 8)
+
+    def centre(g, c):
+        packed = comb[g]
+        inner = beside(s_ref, [(g * 8 + dl) * PAD + 8 for dl in range(8)])
+        for dl in range(8):
+            lev = g * 8 + dl
+            for xt in range(XT):
+                base = lev * PAD + 8 + xt * 8
+                s = s_ref[pl.ds(pl.multiple_of(base, 8), 8), :]
+                total = across(inner, packed, dl * 8 + xt) + s_ref[pl.ds(base - 1, 8), :] + s_ref[pl.ds(base + 1, 8), :]
+                a_ref[lev, xt * 8:xt * 8 + 8, :] = 1.0 - s * total - 2.0 * b_ref[xt * 8:xt * 8 + 8, :]
+        return c
+
+    lax.fori_loop(0, LEV // 8, centre, 0)
+
+    diffuse(0, tr, c_one, u_one, u_two)
     send_halos(1, u_two)
 
     def scatter_rows(i, c):
@@ -391,7 +392,6 @@
             v = jnp.where(live(o, q * 128, 128), v, 0.0)
             index = cols[o, :, q * 128:q * 128 + 128]
             to = slice((o * 4 + q) * 128, (o * 4 + q) * 128 + 128)
-            onehot_s[:, to] = onehot_rows(index & 255, 256)
             spread_s[:, to] = spread(split_pair(v), index >> 8, 8)
     ends = lax.dot_general(
         spread_s[...], onehot_s[...], (((1,), (1,)), ((), ())), preferred_element_type=F32)

time: 44.9 us -> 43.9 us (0.978)
  Pallas kernels: 42.2 us -> 41.2 us
    pallas_call x1, Pallas kernels: 42.2 us -> 41.2 us  [per_device(): pl.pallas_call(kernel, out_shape=(pltpu.VMEM((4, AC), F32), pltpu.VMEM((2...]
where the time goes in v4:
time: 43.9 us; the launch traced here: 43.8 us
  Pallas kernels  41.2 us (94%)
  local copies, waits for them, and re-layouts  1.94 us (4%)
  between operations  0.64 us (1%)
    pallas_call x1, Pallas kernels, per_device(): pl.pallas_call(kernel, out_shape=(pltpu.VMEM((4, AC), F32), pltpu.VMEM((2...  41.2 us
    unnamed x2, local copies, waits for them, and re-layouts  1.94 us

profile of v4, /device:TPU:105, one launch (start us, length us, event | category | flops | bytes accessed | tf_op | source)
XLA Modules:
  0.0 43.8 jit_solution(2337794834898811027)
XLA Ops:
  0.6 41.2 %couple.1 = (f32[4,2048]{1,0:T(4,128)S(1)}, f32[2,32,64,128]{3,2,1,0:T(8,128)S(1)}) custom-call(s32[1,9]{1,0:T(1,128)} %pc_ref.1, f32[8,2048]{1,0:T(8,128)} %atm_hbm.1, s32[9,1,512]{2,1,0:T(1,128)} %bitcast.1, s32[4,64,128]{2,1,0:T(8,128)} %slot_hbm.1, f32[4,64,128]{2,1,0:T(8,128)} %weight_hbm.1, s32[64,128]{1,0:T(8,128)} %land_hbm.1, ...), custom_call_target="tpu_custom_call" | custom-call | tf_op jit(solution)/shard_map/couple/pallas_call | solution.py:411
  41.8 0.6 %copy.12 = f32[4,2048]{1,0:T(4,128)} copy(f32[4,2048]{1,0:T(4,128)S(1)} %get-tuple-element.2) | data formatting | bytes 65536
  42.5 1.3 %copy.13 = f32[2,32,64,128]{3,2,1,0:T(8,128)} copy(f32[2,32,64,128]{3,2,1,0:T(8,128)S(1)} %get-tuple-element.3) | data formatting | bytes 4194304

commit v5 on v4

--- a/solution.py
+++ b/solution.py
@@ -13,7 +13,7 @@
 OFFSETS = [(o // 3 - 1, o % 3 - 1) for o in range(9)]
 AROUND = [o for o in range(9) if o != 4]
 XT = CX // 8
-GROUPS = LEV // 4
+GROUPS = LEV // 8
 GX, SX = 16, 16
 PAD = CX + 16
 
@@ -84,13 +84,15 @@
         @pl.when(missing)
         def _():
             for step in range(STEPS):
-                xrecv[step, side] = jnp.zeros((2 * LEV, CY), F32)
+                for t in range(2):
+                    xrecv[step, t, side] = jnp.zeros((LEV, CY), F32)
             sxrecv[side] = jnp.zeros((LEV, CY), F32)
     for side, missing in ((0, gy == 0), (1, gy == n_gy - 1)):
         @pl.when(missing)
         def _():
             for step in range(STEPS):
-                yrecv[step, side] = jnp.zeros((GROUPS, 8, 128), F32)
+                for t in range(2):
+                    yrecv[step, t, side] = jnp.zeros((GROUPS, 8, 128), F32)
             syrecv[side] = jnp.zeros((LEV // 8, 8, 128), F32)
 
     def live(o, base, width):
@@ -113,15 +115,17 @@
             else:
                 psend[o, :, q * 128:q * 128 + 128] = r
 
-    def edge_rows(src, dst, levels):
-        for j in range(levels // 8):
-            dst[0, j * 8:j * 8 + 8, :] = src[pl.ds(j * 8 * PAD + 8 + CX - 1, 8, stride=PAD), :]
-            dst[1, j * 8:j * 8 + 8, :] = src[pl.ds(j * 8 * PAD + 8, 8, stride=PAD), :]
-
-    def halo_rows(src, dst, levels):
-        for j in range(levels // 8):
-            dst[pl.ds(j * 8 * PAD + 7, 8, stride=PAD), :] = src[0, j * 8:j * 8 + 8, :]
-            dst[pl.ds(j * 8 * PAD + 8 + CX, 8, stride=PAD), :] = src[1, j * 8:j * 8 + 8, :]
+    def edge_rows(src, dst, t=0):
+        for j in range(LEV // 8):
+            base = (t * LEV + j * 8) * PAD + 8
+            dst[0, j * 8:j * 8 + 8, :] = src[pl.ds(base + CX - 1, 8, stride=PAD), :]
+            dst[1, j * 8:j * 8 + 8, :] = src[pl.ds(base, 8, stride=PAD), :]
+
+    def halo_rows(src, dst, t=0):
+        for j in range(LEV // 8):
+            base = (t * LEV + j * 8) * PAD + 8
+            dst[pl.ds(base - 1, 8, stride=PAD), :] = src[0, j * 8:j * 8 + 8, :]
+            dst[pl.ds(base + CX, 8, stride=PAD), :] = src[1, j * 8:j * 8 + 8, :]
 
     def halo_copies(xs, xr, ys, yr, n):
         made = []
@@ -184,40 +188,40 @@
         return c
 
     lax.fori_loop(0, LEV // 8, start_s, 0)
-    edge_rows(s_ref, sxsend, LEV)
-    s_halos = halo_copies(sxsend, sxrecv, sysend, syrecv, STEPS)
+    edge_rows(s_ref, sxsend)
+    s_halos = halo_copies(sxsend, sxrecv, sysend, syrecv, 2 * STEPS)
     start(s_halos)
 
-    def edge_columns(src, dst, g, c):
+    def edge_columns(src, t, dst, g, c):
         acc = jnp.zeros((8, 128), F32)
-        for dl in range(4):
-            lev = g * 4 + dl
-            for t in range(2):
-                for xt in range(XT):
-                    base = (t * LEV + lev) * PAD + 8 + xt * 8
-                    acc = edge(acc, src[pl.ds(pl.multiple_of(base, 8), 8), :], dl * 16 + t * 8 + xt)
+        for dl in range(8):
+            lev = g * 8 + dl
+            for xt in range(XT):
+                base = (t * LEV + lev) * PAD + 8 + xt * 8
+                acc = edge(acc, src[pl.ds(pl.multiple_of(base, 8), 8), :], dl * 8 + xt)
         dst[g] = acc
         return c
 
-    def start_u(g, c):
+    def start_u(t, g, c):
         acc = jnp.zeros((8, 128), F32)
-        for dl in range(4):
-            lev = g * 4 + dl
+        for dl in range(8):
+            lev = g * 8 + dl
             for xt in range(XT):
                 s = s_ref[pl.ds(pl.multiple_of(lev * PAD + 8 + xt * 8, 8), 8), :]
-                for t in range(2):
-                    u = s * tr[t, lev, xt * 8:xt * 8 + 8, :]
-                    u_one[pl.ds(pl.multiple_of((t * LEV + lev) * PAD + 8 + xt * 8, 8), 8), :] = u
-                    acc = edge(acc, u, dl * 16 + t * 8 + xt)
-        ysend[0, g] = acc
+                u = s * tr[t, lev, xt * 8:xt * 8 + 8, :]
+                u_one[pl.ds(pl.multiple_of((t * LEV + lev) * PAD + 8 + xt * 8, 8), 8), :] = u
+                acc = edge(acc, u, dl * 8 + xt)
+        ysend[0, t, g] = acc
         return c
 
+    u_halos = [
+        [halo_copies(xsend.at[n, t], xrecv.at[n, t], ysend.at[n, t], yrecv.at[n, t], 2 * n + t) for t in range(2)]
+        for n in range(STEPS)]
     loads[5].wait()
-    lax.fori_loop(0, GROUPS, start_u, 0)
-
-    edge_rows(u_one, xsend.at[0], 2 * LEV)
-    u_halos = [halo_copies(xsend.at[n], xrecv.at[n], ysend.at[n], yrecv.at[n], n) for n in range(STEPS)]
-    start(u_halos[0])
+    for t in range(2):
+        lax.fori_loop(0, GROUPS, functools.partial(start_u, t), 0)
+        edge_rows(u_one, xsend.at[0, t], t)
+        start(u_halos[0][t])
 
     def columns_in(src, groups):
         for g in range(groups):
@@ -241,39 +245,42 @@
 
     at_end = (lane == 0) | (lane == 127)
 
-    def diffuse(step, c_src, c_dst, u_src, u_dst):
-        received(u_halos[step])
-        halo_rows(xrecv.at[step], u_src, 2 * LEV)
-        columns_in(yrecv.at[step], GROUPS)
+    def diffuse_one(step, t, c_src, c_dst, u_src, u_dst):
+        received(u_halos[step][t])
+        halo_rows(xrecv.at[step, t], u_src, t)
+        columns_in(yrecv.at[step, t], GROUPS)
+        last = step == STEPS - 1
 
         def group(g, c):
             packed = comb[g]
-            inner = beside(u_src, [(t * LEV + g * 4 + dl) * PAD + 8 for dl in range(4) for t in range(2)])
+            inner = beside(u_src, [(t * LEV + g * 8 + dl) * PAD + 8 for dl in range(8)])
             added = jnp.minimum(g, 1)
-            for dl in range(4):
-                lev = g * 4 + dl
+            for dl in range(8):
+                lev = g * 8 + dl
                 above, below = jnp.maximum(lev - 1, 0), jnp.minimum(lev + 1, LEV - 1)
                 for xt in range(XT):
                     at = slice(xt * 8, xt * 8 + 8)
                     s = s_ref[pl.ds(pl.multiple_of(lev * PAD + 8 + xt * 8, 8), 8), :]
-                    a, b = a_ref[lev, at, :], b_ref[at, :]
-                    for t in range(2):
-                        base = (t * LEV + lev) * PAD + 8 + xt * 8
-                        total = across(inner, packed, dl * 16 + t * 8 + xt) + u_src[pl.ds(base - 1, 8), :] + u_src[pl.ds(base + 1, 8), :]
-                        new = a * c_src[t, lev, at, :] + s * total + b * (c_src[t, above, at, :] + c_src[t, below, at, :])
-                        if dl == 0:
-                            new = new + force[added, t, at, :]
-                        c_dst[t, lev, at, :] = new
-                        if step < STEPS - 1:
-                            u_dst[pl.ds(pl.multiple_of(base, 8), 8), :] = s * new
+                    base = (t * LEV + lev) * PAD + 8 + xt * 8
+                    total = across(inner, packed, dl * 8 + xt) + u_src[pl.ds(base - 1, 8), :] + u_src[pl.ds(base + 1, 8), :]
+                    new = a_ref[lev, at, :] * c_src[t, lev, at, :] + s * total
+                    new = new + b_ref[at, :] * (c_src[t, above, at, :] + c_src[t, below, at, :])
+                    if dl == 0:
+                        new = new + force[added, t, at, :]
+                    c_dst[t, lev, at, :] = new
+                    if not last:
+                        u_dst[pl.ds(pl.multiple_of(base, 8), 8), :] = s * new
             return c
 
         lax.fori_loop(0, GROUPS, group, 0)
-
-    def send_halos(step, src):
-        lax.fori_loop(0, GROUPS, functools.partial(edge_columns, src, ysend.at[step]), 0)
-        edge_rows(src, xsend.at[step], 2 * LEV)
-        start(u_halos[step])
+        if not last:
+            lax.fori_loop(0, GROUPS, functools.partial(edge_columns, u_dst, t, ysend.at[step + 1, t]), 0)
+            edge_rows(u_dst, xsend.at[step + 1, t], t)
+            start(u_halos[step + 1][t])
+
+    def diffuse(*step):
+        for t in range(2):
+            diffuse_one(step[0], t, *step[1:])
 
     for xt in range(XT):
         at = slice(xt * 8, xt * 8 + 8)
@@ -329,7 +336,7 @@
         force[1, 1, at, :] = jnp.zeros((8, CY), F32)
 
     received(s_halos)
-    halo_rows(sxrecv, s_ref, LEV)
+    halo_rows(sxrecv, s_ref)
     columns_in(syrecv, LEV // 8)
 
     def centre(g, c):
@@ -347,7 +354,6 @@
     lax.fori_loop(0, LEV // 8, centre, 0)
 
     diffuse(0, tr, c_one, u_one, u_two)
-    send_halos(1, u_two)
 
     def scatter_rows(i, c):
         hots, spreads = [], []
@@ -363,10 +369,8 @@
 
     back = lax.fori_loop(0, 2, scatter_rows, jnp.zeros((256, 144), F32))
     diffuse(1, c_one, c_two, u_two, u_one)
-    send_halos(2, u_one)
     back = scatter_rows(2, back)
     diffuse(2, c_two, c_one, u_one, u_two)
-    send_halos(3, u_two)
     back = scatter_rows(3, back).T
     for o in range(9):
         for half in range(2):
@@ -401,8 +405,9 @@
     sent(packs)
     sent(s_halos)
     sent(backs)
-    for copies in u_halos:
-        sent(copies)
+    for pair in u_halos:
+        for copies in pair:
+            sent(copies)
 
 
 def per_device(atm_fields, send_cols, pair_count, remap_slot, remap_weight, land_mask, tracers, kappa):
@@ -425,11 +430,11 @@
             V((2, LEV, CX, CY), F32), V((2, LEV, CX, CY), F32),
             V((2 * LEV * PAD, CY), F32), V((2 * LEV * PAD, CY), F32), V((GROUPS, 8, 128), F32),
             V((64, 36 * 128), BF16), V((256, 36 * 128), BF16), V((2, 144, 256), BF16), V((256, 128), BF16),
-            V((STEPS, 2, 2 * LEV, CY), F32), V((STEPS, 2, 2 * LEV, CY), F32),
-            V((STEPS, GROUPS, 8, 128), F32), V((STEPS, 2, GROUPS, 8, 128), F32),
+            V((STEPS, 2, 2, LEV, CY), F32), V((STEPS, 2, 2, LEV, CY), F32),
+            V((STEPS, 2, GROUPS, 8, 128), F32), V((STEPS, 2, 2, GROUPS, 8, 128), F32),
             V((2, LEV, CY), F32), V((2, LEV, CY), F32), V((LEV // 8, 8, 128), F32), V((2, LEV // 8, 8, 128), F32),
             S.DMA((7,)), S.DMA((9,)), S.DMA((9,)), S.DMA((9,)), S.DMA((9,)),
-            S.DMA((STEPS + 1, 4)), S.DMA((STEPS + 1, 4)),
+            S.DMA((2 * STEPS + 1, 4)), S.DMA((2 * STEPS + 1, 4)),
         ],
         compiler_params=pltpu.CompilerParams(
             collective_id=0, has_side_effects=True, vmem_limit_bytes=52 << 20),

time: 43.9 us -> 40.7 us (0.927)
  Pallas kernels: 41.2 us -> 38 us
    pallas_call x1, Pallas kernels: 41.2 us -> 38 us  [per_device(): pl.pallas_call(kernel, out_shape=(pltpu.VMEM((4, AC), F32), pltpu.VMEM((2...]
where the time goes in v5:
time: 40.7 us; the launch traced here: 40.6 us
  Pallas kernels  38 us (93%)
  local copies, waits for them, and re-layouts  1.94 us (5%)
  between operations  0.64 us (2%)
    pallas_call x1, Pallas kernels, per_device(): pl.pallas_call(kernel, out_shape=(pltpu.VMEM((4, AC), F32), pltpu.VMEM((2...  38 us
    unnamed x2, local copies, waits for them, and re-layouts  1.94 us

profile of v5, /device:TPU:105, one launch (start us, length us, event | category | flops | bytes accessed | tf_op | source)
XLA Modules:
  0.0 40.6 jit_solution(14533841699546632978)
XLA Ops:
  0.6 38.0 %couple.1 = (f32[4,2048]{1,0:T(4,128)S(1)}, f32[2,32,64,128]{3,2,1,0:T(8,128)S(1)}) custom-call(s32[1,9]{1,0:T(1,128)} %pc_ref.1, f32[8,2048]{1,0:T(8,128)} %atm_hbm.1, s32[9,1,512]{2,1,0:T(1,128)} %bitcast.1, s32[4,64,128]{2,1,0:T(8,128)} %slot_hbm.1, f32[4,64,128]{2,1,0:T(8,128)} %weight_hbm.1, s32[64,128]{1,0:T(8,128)} %land_hbm.1, ...), custom_call_target="tpu_custom_call" | custom-call | tf_op jit(solution)/shard_map/couple/pallas_call | solution.py:416
  38.6 0.6 %copy.12 = f32[4,2048]{1,0:T(4,128)} copy(f32[4,2048]{1,0:T(4,128)S(1)} %get-tuple-element.2) | data formatting | bytes 65536
  39.2 1.3 %copy.13 = f32[2,32,64,128]{3,2,1,0:T(8,128)} copy(f32[2,32,64,128]{3,2,1,0:T(8,128)S(1)} %get-tuple-element.3) | data formatting | bytes 4194304

commit v6 on v5

--- a/solution.py
+++ b/solution.py
@@ -14,7 +14,7 @@
 AROUND = [o for o in range(9) if o != 4]
 XT = CX // 8
 GROUPS = LEV // 8
-GX, SX = 16, 16
+GX, LOOK, SX = 16, 4, 16
 PAD = CX + 16
 
 
@@ -301,9 +301,24 @@
     table_s[0] = head
     table_s[1] = (table - head.astype(F32)).astype(BF16)
 
+    def looked_up(x):
+        acc = jnp.zeros((8, 128), F32)
+        for k in range(K):
+            index = jnp.broadcast_to(slot[k, pl.ds(x, 1), :], (8, 128))
+            low, high = index & 127, index >> 7
+            r = jnp.zeros((8, 128), F32)
+            for h in range(36):
+                part = precv[h // 4, :, h % 4 * 128:h % 4 * 128 + 128]
+                r = jnp.where(high == h, jnp.take_along_axis(part, low, axis=1, mode="promise_in_bounds"), r)
+            acc = acc + jnp.broadcast_to(weight[k, pl.ds(x, 1), :], (8, 128)) * r
+        remap[pl.ds(pl.multiple_of(x * 8, 8), 8), :] = acc
+
     def gather(i, c):
         for xx in range(GX):
             x = i * GX + xx
+            if xx % (GX // LOOK) == 1:
+                looked_up(x)
+                continue
             hot = jnp.concatenate([onehot_rows(slot[k, pl.ds(x, 1), :] & 255, 256) for k in range(K)], 1)
             found = jnp.dot(table_s[0], hot, preferred_element_type=F32) + jnp.dot(table_s[1], hot, preferred_element_type=F32)
             acc = jnp.zeros((8, 128), F32)

time: 40.7 us -> 39.5 us (0.971)
  Pallas kernels: 38 us -> 36.8 us
    pallas_call x1, Pallas kernels: 38 us -> 36.8 us  [per_device(): pl.pallas_call(kernel, out_shape=(pltpu.VMEM((4, AC), F32), pltpu.VMEM((2...]
where the time goes in v6:
time: 39.5 us; the launch traced here: 39.4 us
  Pallas kernels  36.8 us (93%)
  local copies, waits for them, and re-layouts  1.94 us (5%)
  between operations  0.64 us (2%)
    pallas_call x1, Pallas kernels, per_device(): pl.pallas_call(kernel, out_shape=(pltpu.VMEM((4, AC), F32), pltpu.VMEM((2...  36.8 us
    unnamed x2, local copies, waits for them, and re-layouts  1.94 us

profile of v6, /device:TPU:105, one launch (start us, length us, event | category | flops | bytes accessed | tf_op | source)
XLA Modules:
  0.0 39.4 jit_solution(17296503289947394880)
XLA Ops:
  0.6 36.8 %couple.1 = (f32[4,2048]{1,0:T(4,128)S(1)}, f32[2,32,64,128]{3,2,1,0:T(8,128)S(1)}) custom-call(s32[1,9]{1,0:T(1,128)} %pc_ref.1, f32[8,2048]{1,0:T(8,128)} %atm_hbm.1, s32[9,1,512]{2,1,0:T(1,128)} %bitcast.1, s32[4,64,128]{2,1,0:T(8,128)} %slot_hbm.1, f32[4,64,128]{2,1,0:T(8,128)} %weight_hbm.1, s32[64,128]{1,0:T(8,128)} %land_hbm.1, ...), custom_call_target="tpu_custom_call" | custom-call | tf_op jit(solution)/shard_map/couple/pallas_call | solution.py:431
  37.4 0.6 %copy.12 = f32[4,2048]{1,0:T(4,128)} copy(f32[4,2048]{1,0:T(4,128)S(1)} %get-tuple-element.2) | data formatting | bytes 65536
  38.0 1.3 %copy.13 = f32[2,32,64,128]{3,2,1,0:T(8,128)} copy(f32[2,32,64,128]{3,2,1,0:T(8,128)S(1)} %get-tuple-element.3) | data formatting | bytes 4194304

commit v7 on v6

--- a/solution.py
+++ b/solution.py
@@ -14,7 +14,7 @@
 AROUND = [o for o in range(9) if o != 4]
 XT = CX // 8
 GROUPS = LEV // 8
-GX, LOOK, SX = 16, 4, 16
+GX, LOOK, SX = 16, 5, 16
 PAD = CX + 16
 
 

time: 39.5 us -> 39.2 us (level)
  no operation moved by 1% of the time
where the time goes in v7:
time: 39.2 us; the launch traced here: 39.1 us
  Pallas kernels  36.5 us (93%)
  local copies, waits for them, and re-layouts  1.94 us (5%)
  between operations  0.64 us (2%)
    pallas_call x1, Pallas kernels, per_device(): pl.pallas_call(kernel, out_shape=(pltpu.VMEM((4, AC), F32), pltpu.VMEM((2...  36.5 us
    unnamed x2, local copies, waits for them, and re-layouts  1.94 us

profile of v7, /device:TPU:105, one launch (start us, length us, event | category | flops | bytes accessed | tf_op | source)
XLA Modules:
  0.0 39.1 jit_solution(4230569073975615300)
XLA Ops:
  0.6 36.5 %couple.1 = (f32[4,2048]{1,0:T(4,128)S(1)}, f32[2,32,64,128]{3,2,1,0:T(8,128)S(1)}) custom-call(s32[1,9]{1,0:T(1,128)} %pc_ref.1, f32[8,2048]{1,0:T(8,128)} %atm_hbm.1, s32[9,1,512]{2,1,0:T(1,128)} %bitcast.1, s32[4,64,128]{2,1,0:T(8,128)} %slot_hbm.1, f32[4,64,128]{2,1,0:T(8,128)} %weight_hbm.1, s32[64,128]{1,0:T(8,128)} %land_hbm.1, ...), custom_call_target="tpu_custom_call" | custom-call | tf_op jit(solution)/shard_map/couple/pallas_call | solution.py:431
  37.1 0.6 %copy.12 = f32[4,2048]{1,0:T(4,128)} copy(f32[4,2048]{1,0:T(4,128)S(1)} %get-tuple-element.2) | data formatting | bytes 65536
  37.7 1.3 %copy.13 = f32[2,32,64,128]{3,2,1,0:T(8,128)} copy(f32[2,32,64,128]{3,2,1,0:T(8,128)S(1)} %get-tuple-element.3) | data formatting | bytes 4194304
